TPU v7x, 512 devices: a whole 4x8x8 slice. The times are simulated.
512 devices in a mesh: pp: 8 (over x, y_lo), cp: 64 (over y_hi, z, core).
Axes of the slice: x: 4, y: 8 (y_hi: 4, y_lo: 2; y = y_hi * 2 + y_lo), z: 8, core: 2. Of those that a mesh axis runs over, the one named last changes fastest.
Arguments:
- queries: bfloat16 [8, 2, 32, 4096, 128], P('pp', None, None, 'cp'), may hold values from -5 to 5
- keys_values: bfloat16 [8, 2, 2, 4, 4096, 128], P('pp', None, None, None, 'cp'), may hold values from -5 to 5
- old_block: int32 [128], replicated, may hold values from 0 to 127, as said below
- new_block: int32 [128], replicated, may hold values from 0 to 127, as said below
Outputs:
- section_input: bfloat16 [8, 2, 32, 4096, 128], P('pp', None, None, 'cp')
Inputs may be any that keep to these rules, and one draw needn't show every extreme that they name: `old_block`: A permutation of the sequence blocks; row-blocks 4 e to 4 e + 3 hold sequence blocks 2 a, 2 a + 1, 2 b, 2 b + 1 with a + b = 63. `new_block`: A permutation of the sequence blocks; row-blocks 2 d and 2 d + 1 hold sequence blocks c and 127 - c.
All inputs are finite; a program needn't handle non-finite values.
Results may differ from a plain program's by a relative error of at most 0.0098.
Values may be sent and summed in bfloat16 or wider, within the bound.
A program may use at most 64 MiB of HBM per device.

v0:
```python
import math

import jax
import jax.numpy as jnp
from jax import lax
from jax.sharding import PartitionSpec as P


def from_behind(value, axis, steps):
    count = lax.axis_size(axis)
    pairs = [(source, (source + steps) % count) for source in range(count)]
    return lax.ppermute(value, axis, pairs)


def regroup(tensor, block_order):
    dims_shape = tensor.shape
    count_blocks = block_order.shape[0]
    blocked = tensor.reshape(
        dims_shape[:-2] + (count_blocks, dims_shape[-2] // count_blocks, dims_shape[-1])
    )
    picked = jnp.take(blocked, block_order, axis=blocked.ndim - 3)
    return picked.reshape(dims_shape)


def rotate(tensor):
    half_dim = tensor.shape[-1] // 2
    spacing = jnp.arange(half_dim, dtype=jnp.float32) * (2.0 / tensor.shape[-1])
    inverse = jnp.exp(-spacing * jnp.log(jnp.float32(1000000.0)))
    angles = jnp.arange(tensor.shape[-2], dtype=jnp.float32)[:, None] * inverse[None, :]
    cosine = jnp.cos(angles)
    sine_part = jnp.sin(angles)
    widened = tensor.astype(jnp.float32)
    first_half = widened[..., :half_dim]
    second_half = widened[..., half_dim:]
    turned = jnp.concatenate(
        [
            first_half * cosine - second_half * sine_part,
            second_half * cosine + first_half * sine_part,
        ],
        axis=-1,
    )
    return turned.astype(jnp.bfloat16)


def causal_attend(queries, key_rows, value_rows):
    heads_here, length, head_width = queries.shape
    block_rows = min(512, length)
    block_count = length // block_rows
    score_scale = 1.0 / math.sqrt(head_width)
    offsets = jnp.arange(block_rows, dtype=jnp.int32)

    def query_step(query_index, finished):
        first_row = query_index * block_rows
        query_part = lax.dynamic_slice_in_dim(queries, first_row, block_rows, 1)
        query_pos = first_row + offsets

        def key_step(key_index, state_in):
            running, weight_sum, summed = state_in
            key_first = key_index * block_rows
            key_part = lax.dynamic_slice_in_dim(key_rows, key_first, block_rows, 0)
            value_part = lax.dynamic_slice_in_dim(value_rows, key_first, block_rows, 0)
            scores = (
                jnp.einsum("hqd,kd->hqk", query_part, key_part, preferred_element_type=jnp.float32)
                * score_scale
            )
            allowed = (key_first + offsets)[None, :] <= query_pos[:, None]
            scores = jnp.where(allowed[None], scores, -1e30)
            highest = jnp.maximum(running, jnp.max(scores, axis=-1))
            weights = jnp.exp(scores - highest[..., None])
            factor = jnp.exp(running - highest)
            weight_sum = weight_sum * factor + jnp.sum(weights, axis=-1)
            summed = summed * factor[..., None] + jnp.einsum(
                "hqk,kd->hqd",
                weights.astype(jnp.bfloat16),
                value_part,
                preferred_element_type=jnp.float32,
            )
            return (highest, weight_sum, summed)

        initial = (
            jnp.full((heads_here, block_rows), -1e30, jnp.float32),
            jnp.zeros((heads_here, block_rows), jnp.float32),
            jnp.zeros((heads_here, block_rows, head_width), jnp.float32),
        )
        running, weight_sum, summed = lax.fori_loop(0, query_index + 1, key_step, initial)
        output_block = (summed / weight_sum[..., None]).astype(jnp.bfloat16)
        return lax.dynamic_update_slice_in_dim(finished, output_block, first_row, 1)

    return lax.fori_loop(0, block_count, query_step, jnp.zeros(queries.shape, jnp.bfloat16))


def per_device(queries, keys_values, old_block, new_block):
    cp_devices = lax.axis_size("cp")
    sequences = queries.shape[1]
    query_heads = queries.shape[2]
    local_rows = queries.shape[3]
    head_width = queries.shape[4]
    kv_heads = keys_values.shape[3]
    all_items = sequences * query_heads
    items_here = all_items // cp_devices
    sharers = query_heads // kv_heads // items_here
    length = local_rows * cp_devices
    block_count = old_block.shape[0]
    sent_queries = queries.reshape(all_items, local_rows, head_width)
    heard_queries = lax.all_to_all(sent_queries, "cp", split_axis=0, concat_axis=1, tiled=True)
    pairs_local = keys_values.reshape(2, sequences, kv_heads, local_rows, head_width)
    copied = jnp.broadcast_to(
        pairs_local[:, :, :, None], (2, sequences, kv_heads, sharers, local_rows, head_width)
    )
    heard_pairs = lax.all_to_all(
        copied.reshape(2, cp_devices, local_rows, head_width),
        "cp",
        split_axis=1,
        concat_axis=2,
        tiled=True,
    )
    full_pairs = heard_pairs.reshape(2, length, head_width)
    positions = jnp.arange(block_count, dtype=jnp.int32)
    inverse = jnp.zeros((block_count,), jnp.int32).at[old_block].set(positions)
    query_seq = rotate(regroup(heard_queries, inverse))
    key_seq = rotate(regroup(full_pairs[0], inverse))
    value_seq = regroup(full_pairs[1], inverse)
    attended = causal_attend(query_seq, key_seq, value_seq)
    relaid = regroup(attended, new_block)
    returned_here = lax.all_to_all(relaid, "cp", split_axis=1, concat_axis=0, tiled=True)
    returned = from_behind(returned_here, "pp", 1)
    return returned.reshape(1, sequences, query_heads, local_rows, head_width)


def solution(mesh):
    return jax.shard_map(
        per_device,
        mesh=mesh,
        in_specs=(P("pp", None, None, "cp", None), P("pp", None, None, None, "cp", None), P(), P()),
        out_specs=P("pp", None, None, "cp", None),
        check_vma=False,
    )
```

profile of v0, /device:TPU:1, one launch (start us, length us, event | category | flops | bytes accessed | tf_op | source)
XLA Modules:
  0.0 305.9 jit_solution(16460065307012909908)
XLA Ops:
  0.0 17.8 %all-to-all-start = ((bf16[64,64,128]{2,1,0:T(8,128)(2,1)}), bf16[64,64,128]{2,1,0:T(8,128)(2,1)S(1)}, u32[]{:S(2)}, u32[]{:S(2)}) async-start(bf16[64,64,128]{2,1,0:T(8,128)(2,1)} %bitcast.77), calls=%async_computation | async-start | bytes 2097152 | tf_op jit(solution)/shard_map/all_to_all | solution.py:105
  17.8 31.3 %all-to-all-done = bf16[64,64,128]{2,1,0:T(8,128)(2,1)S(1)} async-done(((bf16[64,64,128]{2,1,0:T(8,128)(2,1)}), bf16[64,64,128]{2,1,0:T(8,128)(2,1)S(1)}, u32[]{:S(2)}, u32[]{:S(2)}) %all-to-all-start) | async-done | bytes 1048608 | tf_op jit(solution)/shard_map/all_to_all | solution.py:105
  49.1 1.9 broadcast_in_dim.54
  50.9 8.2 %all-to-all-start.1 = ((bf16[2,64,64,128]{3,2,0,1:T(8,128)(2,1)}), bf16[2,64,64,128]{3,2,0,1:T(8,128)(2,1)S(1)}, u32[]{:S(2)}, u32[]{:S(2)}) async-start(bf16[2,64,64,128]{3,2,0,1:T(8,128)(2,1)} %bitcast.65), calls=%async_computation.1 | async-start | bytes 4194304 | tf_op jit(solution)/shard_map/all_to_all | solution.py:110
  59.2 1.0 scatter_custom_fusion
  60.3 0.6 pad_clamp_fusion
  60.9 0.6 compare_and_fusion
  61.5 2.0 gather_fusion
  63.9 8.8 %subtract_convert_fusion.1 = (bf16[1,4096,64]{2,1,0:T(8,128)(2,1)S(1)}, bf16[1,4096,64]{2,1,0:T(8,128)(2,1)S(1)}) fusion(f32[1,4096,128]{2,1,0:T(8,128)S(1)} %bitcast_convert_fusion.1, f32[64]{0:T(128)S(1)} %multiply_exponential_fusion), kind=kLoop, calls=%fused_computation.33 | loop fusion | flops 2359296 | bytes 3145984 | tf_op jit(solution)/shard_map/convert.4
  72.6 1.5 pad_maximum_fusion
  74.2 52.6 %all-to-all-done.1 = bf16[2,64,64,128]{3,2,0,1:T(8,128)(2,1)S(1)} async-done(((bf16[2,64,64,128]{3,2,0,1:T(8,128)(2,1)}), bf16[2,64,64,128]{3,2,0,1:T(8,128)(2,1)S(1)}, u32[]{:S(2)}, u32[]{:S(2)}) %all-to-all-start.1) | async-done | bytes 2097184 | tf_op jit(solution)/shard_map/all_to_all | solution.py:110
  126.8 1.2 fusion.22
  127.9 0.8 gather_fusion.1
  128.7 0.5 copy-done.1
  129.1 0.8 gather_fusion.2
  130.4 8.6 %subtract_convert_fusion = (bf16[4096,64]{1,0:T(8,128)(2,1)S(1)}, bf16[4096,64]{1,0:T(8,128)(2,1)S(1)}) fusion(f32[4096,128]{1,0:T(8,128)S(1)} %bitcast_convert_fusion, f32[64]{0:T(128)S(1)} %multiply_exponential_fusion), kind=kLoop, calls=%fused_computation.28 | loop fusion | flops 2359296 | bytes 3145984 | tf_op jit(solution)/shard_map/convert.2
  139.0 0.6 pad_maximum_fusion.1
  139.8 45.7 %while.48 = (s32[]{:T(128)}, bf16[1,4096,128]{2,1,0:T(8,128)(2,1)S(1)}, bf16[1,4096,128]{2,1,0:T(8,128)(2,1)}, bf16[4096,128]{1,0:T(8,128)(2,1)S(1)}, bf16[4096,...) while((s32[]{:T(128)}, ...), condition=%wide.region_6.0_spmd.clone.clone, body=%wide.region_1.8_spmd.clone.clone.sunk | while | flops 136579072 | bytes 5032458 | solution.py:89
  139.8 0.9 constant_dynamic-slice_fusion.2
  140.8 1.0 while.49
  142.0 0.9 constant_dynamic-slice_fusion.2
  143.0 2.0 while.49
  144.6 0.4 fusion.34
  145.2 0.9 constant_dynamic-slice_fusion.2
  146.2 3.0 while.49
  148.8 0.4 fusion.34
  149.4 0.9 constant_dynamic-slice_fusion.2
  150.4 4.0 %while.49 = (s32[]{:T(128)}, f32[1,512]{1,0:T(1,128)S(1)}, f32[1,512]{1,0:T(1,128)S(1)}, f32[1,512,128]{2,1,0:T(8,128)S(1)}, s32[]{:T(128)}, /*index=5*/s32[512]...) while((s32[]{:T(128)}, f32[1,512]{1,0:T(1,128)S(1)}, ...), condition=%wide.region_5.7_spmd, body=%wide.region_2.6_spmd.sunk | while | flops 136447488 | bytes 4104383 | solution.py:85
  153.0 0.4 fusion.34
  154.0 0.4 fusion.34
  154.6 0.9 constant_dynamic-slice_fusion.2
  155.6 5.0 %while.49 = (s32[]{:T(128)}, f32[1,512]{1,0:T(1,128)S(1)}, f32[1,512]{1,0:T(1,128)S(1)}, f32[1,512,128]{2,1,0:T(8,128)S(1)}, s32[]{:T(128)}, /*index=5*/s32[512]...) while((s32[]{:T(128)}, f32[1,512]{1,0:T(1,128)S(1)}, ...), condition=%wide.region_5.7_spmd, body=%wide.region_2.6_spmd.sunk | while | flops 136447488 | bytes 4104383 | solution.py:85
  158.2 0.4 fusion.34
  159.2 0.4 fusion.34
  160.2 0.4 fusion.34
  160.8 0.9 constant_dynamic-slice_fusion.2
  161.8 6.0 %while.49 = (s32[]{:T(128)}, f32[1,512]{1,0:T(1,128)S(1)}, f32[1,512]{1,0:T(1,128)S(1)}, f32[1,512,128]{2,1,0:T(8,128)S(1)}, s32[]{:T(128)}, /*index=5*/s32[512]...) while((s32[]{:T(128)}, f32[1,512]{1,0:T(1,128)S(1)}, ...), condition=%wide.region_5.7_spmd, body=%wide.region_2.6_spmd.sunk | while | flops 136447488 | bytes 4104383 | solution.py:85
  164.4 0.4 fusion.34
  165.4 0.4 fusion.34
  166.4 0.4 fusion.34
  167.4 0.4 fusion.34
  168.0 0.9 constant_dynamic-slice_fusion.2
  169.0 7.0 %while.49 = (s32[]{:T(128)}, f32[1,512]{1,0:T(1,128)S(1)}, f32[1,512]{1,0:T(1,128)S(1)}, f32[1,512,128]{2,1,0:T(8,128)S(1)}, s32[]{:T(128)}, /*index=5*/s32[512]...) while((s32[]{:T(128)}, f32[1,512]{1,0:T(1,128)S(1)}, ...), condition=%wide.region_5.7_spmd, body=%wide.region_2.6_spmd.sunk | while | flops 136447488 | bytes 4104383 | solution.py:85
  171.6 0.4 fusion.34
  172.6 0.4 fusion.34
  173.6 0.4 fusion.34
  174.6 0.4 fusion.34
  175.6 0.4 fusion.34
  176.2 0.9 constant_dynamic-slice_fusion.2
  177.2 8.0 %while.49 = (s32[]{:T(128)}, f32[1,512]{1,0:T(1,128)S(1)}, f32[1,512]{1,0:T(1,128)S(1)}, f32[1,512,128]{2,1,0:T(8,128)S(1)}, s32[]{:T(128)}, /*index=5*/s32[512]...) while((s32[]{:T(128)}, f32[1,512]{1,0:T(1,128)S(1)}, ...), condition=%wide.region_5.7_spmd, body=%wide.region_2.6_spmd.sunk | while | flops 136447488 | bytes 4104383 | solution.py:85
  179.8 0.4 fusion.34
  180.8 0.4 fusion.34
  181.8 0.4 fusion.34
  182.8 0.4 fusion.34
  183.8 0.4 fusion.34
  185.4 0.9 gather_fusion.3
  186.6 16.7 %copy.10 = bf16[1,4096,128]{2,0,1:T(2,128)(2,1)S(1)} copy(bf16[1,4096,128]{2,1,0:T(8,128)(2,1)S(1)} %bitcast.69) | data formatting | bytes 2097152 | tf_op jit(solution)/shard_map/reshape | solution.py:22
  203.3 0.5 broadcast.145
  203.8 22.4 %reduce.4 = bf16[4096,128]{1,0:T(8,128)(2,1)S(1)} reduce(bf16[4096,1,128]{2,1,0:T(2,128)(2,1)S(1)} %bitcast.66, bf16[]{:T(256)} %broadcast.145), dimensions={1}, to_apply=%bitcast.46.reduce_sub_computation | reduce | bytes 2097154
  226.5 48.5 %all_to_all.30 = bf16[64,2,4096]{2,1,0:T(2,128)(2,1)S(1)} all-to-all(bf16[64,2,4096]{2,1,0:T(2,128)(2,1)S(1)} %reshape.272), channel_id=1, replica_groups=mesh['pp'=8,'cp'=64] {'cp'}, dimensions={0} | all-to-all | bytes 2097152 | tf_op jit(solution)/shard_map/all_to_all | solution.py:125
  275.0 1.0 reshape.273
  276.2 1.9 collective-permute-start
  278.2 26.8 %collective-permute-done = bf16[64,64,128]{2,1,0:T(8,128)(2,1)S(1)} collective-permute-done((bf16[64,64,128]{2,1,0:T(8,128)(2,1)S(1)}, bf16[64,64,128]{2,1,0:T(8,128)(2,1)S(1)}, u32[]{:S(2)}, u32[]{:S(2)}) %collective-permute-start) | collective-permute-done | bytes 1048608 | tf_op jit(solution)/shard_map/ppermute | solution.py:12
  305.0 1.0 copy.33
  (306 shorter events, 29.1 us)
Async XLA Ops:
  0.0 17.8 %copy-start.2 = (bf16[1,2,2,4,64,128]{5,4,3,2,1,0:T(8,128)(2,1)S(1)}, bf16[1,2,2,4,64,128]{5,4,3,2,1,0:T(8,128)(2,1)}, u32[]{:S(2)}) copy-start(bf16[1,2,2,4,64,128]{5,4,3,2,1,0:T(8,128)(2,1)} %param.13) | copy-start | bytes 786436
  0.0 49.1 %all-to-all-start = ((bf16[64,64,128]{2,1,0:T(8,128)(2,1)}), bf16[64,64,128]{2,1,0:T(8,128)(2,1)S(1)}, u32[]{:S(2)}, u32[]{:S(2)}) async-start(bf16[64,64,128]{2,1,0:T(8,128)(2,1)} %bitcast.77), calls=%async_computation | async-start | bytes 2097152 | tf_op jit(solution)/shard_map/all_to_all | solution.py:105
  49.1 1.9 copy-start
  50.9 8.3 %copy-start.4 = (s32[128]{0:T(128)S(1)}, s32[128]{0:T(128)}, u32[]{:S(2)}) copy-start(s32[128]{0:T(128)} %param.14) | copy-start | bytes 1540
  50.9 9.3 %copy-start.5 = (s32[128]{0:T(128)S(1)}, s32[128]{0:T(128)}, u32[]{:S(2)}) copy-start(s32[128]{0:T(128)} %param.15) | copy-start | bytes 1540
  50.9 75.8 %all-to-all-start.1 = ((bf16[2,64,64,128]{3,2,0,1:T(8,128)(2,1)}), bf16[2,64,64,128]{3,2,0,1:T(8,128)(2,1)S(1)}, u32[]{:S(2)}, u32[]{:S(2)}) async-start(bf16[2,64,64,128]{3,2,0,1:T(8,128)(2,1)} %bitcast.65), calls=%async_computation.1 | async-start | bytes 4194304 | tf_op jit(solution)/shard_map/all_to_all | solution.py:110
  127.9 1.2 copy-start.1
  185.4 0.9 copy-start.3
  276.2 28.7 %collective-permute-start = (bf16[64,64,128]{2,1,0:T(8,128)(2,1)S(1)}, bf16[64,64,128]{2,1,0:T(8,128)(2,1)S(1)}, u32[]{:S(2)}, u32[]{:S(2)}) collective-permute-start(bf16[64,64,128]{2,1,0:T(8,128)(2,1)S(1)} %bitcast.76), channel_id=1, source_target_pairs={{0,64},{64,128},{128,192},{192,256},{256,320},{320,384},{384,448},... | collective-permute-start | bytes 3145736 | tf_op jit(solution)/shard_map/ppermute | solution.py:12
where the time goes:
time: 307 us; the launch traced here: 306 us
  waiting for transfers between devices  111 us (36%)
  other arithmetic  53.7 us (17%)
  blocking collectives  48.5 us (16%)
  local copies, waits for them, and re-layouts  36.4 us (12%)
  starting transfers between devices  27.9 us (9%)
  matrix products  25.8 us (8%)
    all_to_all x1, waiting for transfers between devices, per_device(): lax.all_to_all(copied.reshape(2, cp_devices, local_rows, head_width), 'cp...  52.6 us
    all_to_all x1, blocking collectives, per_device(): lax.all_to_all(relaid, 'cp', split_axis=1, concat_axis=0, tiled=True)  48.5 us
    all_to_all x1, waiting for transfers between devices, per_device(): lax.all_to_all(sent_queries, 'cp', split_axis=0, concat_axis=1, tiled=True)  31.3 us
    ppermute x1, waiting for transfers between devices, from_behind(): return lax.ppermute(value, axis, pairs)  26.8 us
    unnamed x1, other arithmetic  22.4 us
    all_to_all x1, starting transfers between devices, per_device(): lax.all_to_all(sent_queries, 'cp', split_axis=0, concat_axis=1, tiled=True)  17.8 us
    another operation x2, other arithmetic  17.3 us
    reshape x1, local copies, waits for them, and re-layouts, regroup(): return picked.reshape(dims_shape)  16.7 us
  transfers between devices with their start and end apart: 3, of which 3 were waited for; matrix products, arithmetic and copies ran while one was open for 5% of the time, Pallas kernels for 0%

commit v1 on v0

v1 whole, which is shorter than its diff:
```python
import functools
import math
import random

import jax
import jax.numpy as jnp
from jax import lax
from jax.experimental import pallas as pl
from jax.experimental.pallas import tpu as pltpu
from jax.sharding import PartitionSpec as P

MESH = pl.DeviceIdType.MESH
F32 = jnp.float32
BF16 = jnp.bfloat16
LENGTH = 4096
DIM = 128
BLOCKS = 128
ROWS = 32
LOCAL = 64
YS, ZS = 4, 8
SECTIONS = 8
VROWS = 144


def steps_of(seed):
    steps = [(dy, dz, dc) for dy in range(YS) for dz in range(ZS) for dc in range(2)]
    random.Random(seed).shuffle(steps)
    return steps


def place():
    me = lax.axis_index("cp")
    return me // 16, lax.rem(me // 2, ZS), lax.rem(me, 2)


def at(dy, dz, dc):
    y, z, c = place()
    return lax.rem(y + dy, YS) * 16 + lax.rem(z + dz, ZS) * 2 + lax.rem(c + dc, 2)


def turned(x, cos, sin):
    wide = x.astype(F32)
    return (wide * cos + pltpu.roll(wide, 64, wide.ndim - 1) * sin).astype(BF16)


def gather_kernel(
    q_ref, kv_ref, cos_ref, sin_ref, oq_ref, okv_ref, qs, kvs,
    q_send, q_recv, z_send, z_recv, y_send, y_recv, c_send, c_recv, loc,
):
    pp = lax.axis_index("pp")
    me = lax.axis_index("cp")
    y, z, c = place()
    steps = [s for s in steps_of(1) if s != (0, 0, 0)]
    barrier = pltpu.get_barrier_semaphore()
    for s in steps:
        pl.semaphore_signal(barrier, inc=1, device_id=(pp, at(*s)), device_id_type=MESH)
    cos, sin = cos_ref[...], sin_ref[...]

    def turn_keys(j, carry):
        kvs[0, j] = turned(kv_ref[0, j], cos, sin)
        kvs[1, j] = kv_ref[1, j]
        return carry

    lax.fori_loop(0, 8, turn_keys, 0)
    pl.semaphore_wait(barrier, len(steps))

    def remote(src, dst, send, recv, dev):
        copy = pltpu.make_async_remote_copy(
            src_ref=src, dst_ref=dst, send_sem=send, recv_sem=recv,
            device_id=(pp, dev), device_id_type=MESH,
        )
        copy.start()
        return copy

    z_copies = []
    for n, dz in enumerate((4, 3, 5, 2, 6, 1, 7)):
        z_copies.append(remote(
            kvs.at[:, lax.rem(z + dz, ZS)], okv_ref.at[:, y, c, z],
            z_send.at[n], z_recv.at[n], at(0, dz, 0),
        ))
    own = pltpu.make_async_copy(kvs.at[:, z], okv_ref.at[:, y, c, z], loc.at[0])
    own.start()

    q_copies = []

    def send_queries(first, last):
        for n in range(first, last):
            d = at(*steps[n])
            dy, dz, dc = steps[n]
            item = lax.rem(z + dz, ZS) * 8 + lax.rem(y + dy, YS) * 2 + lax.rem(c + dc, 2)
            qs[item] = turned(q_ref[item], cos, sin)
            q_copies.append(remote(qs.at[item], oq_ref.at[me], q_send.at[n], q_recv.at[n], d))

    send_queries(0, 20)
    mine = z * 8 + y * 2 + c
    qs[mine] = turned(q_ref[mine], cos, sin)
    own_q = pltpu.make_async_copy(qs.at[mine], oq_ref.at[me], loc.at[1])
    own_q.start()

    for copy in z_copies:
        copy.wait_recv()
    own.wait()
    mine_kv = okv_ref.at[:, y, c]
    up = remote(mine_kv, mine_kv, y_send.at[0], y_recv.at[0], at(1, 0, 0))
    down = remote(mine_kv, mine_kv, y_send.at[1], y_recv.at[1], at(YS - 1, 0, 0))
    core = [remote(mine_kv, mine_kv, c_send.at[0], c_recv.at[0], at(0, 0, 1))]
    send_queries(20, 42)
    below, above, far = lax.rem(y + 3, YS), lax.rem(y + 1, YS), lax.rem(y + 2, YS)
    up.wait_recv()
    keys = okv_ref.at[0, below, c]
    up2 = remote(keys, keys, y_send.at[2], y_recv.at[2], at(1, 0, 0))
    part = okv_ref.at[:, below, c]
    core.append(remote(part, part, c_send.at[1], c_recv.at[1], at(0, 0, 1)))
    down.wait_recv()
    values = okv_ref.at[1, above, c]
    down2 = remote(values, values, y_send.at[3], y_recv.at[3], at(YS - 1, 0, 0))
    part = okv_ref.at[:, above, c]
    core.append(remote(part, part, c_send.at[2], c_recv.at[2], at(0, 0, 1)))
    send_queries(42, 63)
    up2.wait_recv()
    down2.wait_recv()
    part = okv_ref.at[:, far, c]
    core.append(remote(part, part, c_send.at[3], c_recv.at[3], at(0, 0, 1)))
    own_q.wait()
    for copy in q_copies + core:
        copy.wait()
    for copy in z_copies + [up, down, up2, down2]:
        copy.wait_send()


def gather(queries, pairs, cos, sin):
    vmem = pl.BlockSpec(memory_space=pltpu.VMEM)
    hbm = pl.BlockSpec(memory_space=pl.ANY)
    dma = pltpu.SemaphoreType.DMA
    return pl.pallas_call(
        gather_kernel,
        out_shape=(
            jax.ShapeDtypeStruct((64, LOCAL, DIM), BF16),
            jax.ShapeDtypeStruct((2, YS, 2, ZS, LOCAL, DIM), BF16),
        ),
        in_specs=[vmem] * 4,
        out_specs=(hbm, hbm),
        scratch_shapes=[
            pltpu.VMEM((64, LOCAL, DIM), BF16),
            pltpu.VMEM((2, 8, LOCAL, DIM), BF16),
            dma((63,)), dma((63,)), dma((7,)), dma((7,)), dma((4,)), dma((4,)), dma((4,)), dma((4,)), dma((2,)),
        ],
        compiler_params=pltpu.CompilerParams(
            collective_id=1, has_side_effects=True, vmem_limit_bytes=24 * 2**20
        ),
        name="gather",
    )(queries, pairs, cos, sin)


def scatter_kernel(x_ref, o_ref, send, recv):
    pp = lax.axis_index("pp")
    ahead, behind = lax.rem(pp + 1, SECTIONS), lax.rem(pp + SECTIONS - 1, SECTIONS)
    y, z, c = place()
    item = z * 8 + y * 2 + c
    steps = steps_of(2)
    barrier = pltpu.get_barrier_semaphore()
    for s in steps:
        pl.semaphore_signal(barrier, inc=1, device_id=(behind, at(*s)), device_id_type=MESH)
    pl.semaphore_wait(barrier, len(steps))
    copies = []
    for n, s in enumerate(steps):
        d = at(*s)
        copy = pltpu.make_async_remote_copy(
            src_ref=x_ref.at[d], dst_ref=o_ref.at[item], send_sem=send.at[n], recv_sem=recv.at[n],
            device_id=(ahead, d), device_id_type=MESH,
        )
        copy.start()
        copies.append(copy)
    for copy in copies:
        copy.wait()


def scatter(relaid):
    hbm = pl.BlockSpec(memory_space=pl.ANY)
    return pl.pallas_call(
        scatter_kernel,
        out_shape=jax.ShapeDtypeStruct((64, LOCAL, DIM), BF16),
        in_specs=[hbm],
        out_specs=hbm,
        scratch_shapes=[pltpu.SemaphoreType.DMA((64,)), pltpu.SemaphoreType.DMA((64,))],
        compiler_params=pltpu.CompilerParams(
            collective_id=2, has_side_effects=True, vmem_limit_bytes=24 * 2**20
        ),
        name="scatter",
    )(relaid)


def key_row_block(j):
    device = j // 2
    y, z, c = device // 16, lax.rem(device // 2, ZS), lax.rem(device, 2)
    return ((y * 2 + c) * ZS + z) * 2 + lax.rem(j, 2)


def attend_kernel(old_ref, new_ref, q_ref, kv_ref, o_ref, qs, k2, vt, qt, oseq, acc, mx, *, bq, bk):
    scale = math.log2(math.e) / math.sqrt(DIM)

    def arrange(j, carry):
        dst = pl.ds(pl.multiple_of(old_ref[j] * ROWS, ROWS), ROWS)
        src = pl.ds(pl.multiple_of(key_row_block(j) * ROWS, ROWS), ROWS)
        keys = kv_ref[0, src, :]
        k2[dst, 0:DIM] = keys
        k2[dst, DIM : 2 * DIM] = keys
        qs[dst, :] = q_ref[pl.ds(pl.multiple_of(j * ROWS, ROWS), ROWS), :]
        oseq[dst, :] = kv_ref[1, src, :]
        return carry

    lax.fori_loop(0, BLOCKS, arrange, 0, unroll=8)

    def turn(j, carry):
        rows = pl.ds(pl.multiple_of(j * 512, 512), 512)
        x = qs[rows, :].astype(F32) * scale
        high = x.astype(BF16)
        low = (x - high.astype(F32)).astype(BF16)
        qt[0:DIM, rows] = high.T
        qt[DIM : 2 * DIM, rows] = low.T
        vt[0:DIM, rows] = oseq[rows, :].T
        vt[DIM:VROWS, rows] = jnp.ones((VROWS - DIM, 512), BF16)
        return carry

    lax.fori_loop(0, LENGTH // 512, turn, 0)

    def query_step(i, carry):
        q0 = pl.multiple_of(i * bq, bq)

        def block(k0, width, first):
            s = jnp.dot(k2[pl.ds(k0, width), :], qt[:, pl.ds(q0, bq)], preferred_element_type=F32)
            if first:
                key = lax.broadcasted_iota(jnp.int32, s.shape, 0)
                query = lax.broadcasted_iota(jnp.int32, s.shape, 1)
                s = jnp.where(key <= query, s, -1e30)
            top = jnp.max(s, axis=0, keepdims=True)
            if not first:
                before = mx[...]
                top = jnp.maximum(before, top)
            weights = jnp.exp2(s - top).astype(BF16)
            summed = jnp.dot(vt[:, pl.ds(k0, width)], weights, preferred_element_type=F32)
            if not first:
                summed = acc[...] * jnp.exp2(before - top) + summed
            acc[...] = summed
            mx[...] = top

        block(q0, bq, True)

        def body(j, inner):
            block(pl.multiple_of(j * bk, bk), bk, False)
            return inner

        lax.fori_loop(0, i * bq // bk, body, 0)
        oseq[pl.ds(q0, bq), :] = (acc[0:DIM, :] / acc[DIM : DIM + 1, :]).T.astype(BF16)
        return carry

    lax.fori_loop(0, LENGTH // bq, query_step, 0)

    def relay(j, carry):
        src = pl.ds(pl.multiple_of(new_ref[j] * ROWS, ROWS), ROWS)
        o_ref[pl.ds(pl.multiple_of(j * ROWS, ROWS), ROWS), :] = oseq[src, :]
        return carry

    lax.fori_loop(0, BLOCKS, relay, 0, unroll=8)


def attend(old_block, new_block, queries, pairs, bq=1024, bk=1024):
    vmem = pl.BlockSpec(memory_space=pltpu.VMEM)
    smem = pl.BlockSpec(memory_space=pltpu.SMEM)
    return pl.pallas_call(
        functools.partial(attend_kernel, bq=bq, bk=bk),
        out_shape=jax.ShapeDtypeStruct((LENGTH, DIM), BF16),
        in_specs=[smem, smem, vmem, vmem],
        out_specs=vmem,
        scratch_shapes=[
            pltpu.VMEM((LENGTH, DIM), BF16),
            pltpu.VMEM((LENGTH, 2 * DIM), BF16),
            pltpu.VMEM((VROWS, LENGTH), BF16),
            pltpu.VMEM((2 * DIM, LENGTH), BF16),
            pltpu.VMEM((LENGTH, DIM), BF16),
            pltpu.VMEM((VROWS, bq), F32),
            pltpu.VMEM((1, bq), F32),
        ],
        compiler_params=pltpu.CompilerParams(vmem_limit_bytes=48 * 2**20),
        name="attend",
    )(old_block, new_block, queries, pairs)


def per_device(queries, keys_values, old_block, new_block):
    me = lax.axis_index("cp")
    two = lax.dynamic_slice_in_dim(old_block, me * 2, 2)
    token = (two[:, None] * ROWS + jnp.arange(ROWS, dtype=jnp.int32)[None, :]).reshape(LOCAL)
    spacing = jnp.arange(DIM // 2, dtype=F32) * (2.0 / DIM)
    inverse = jnp.exp(-spacing * jnp.log(F32(1000000.0)))
    angles = token.astype(F32)[:, None] * inverse[None, :]
    cosine, sine = jnp.cos(angles), jnp.sin(angles)
    cos = jnp.concatenate([cosine, cosine], axis=1)
    sin = jnp.concatenate([-sine, sine], axis=1)
    all_queries, pairs = gather(
        queries.reshape(64, LOCAL, DIM), keys_values.reshape(2, 8, LOCAL, DIM), cos, sin
    )
    relaid = attend(
        old_block, new_block, all_queries.reshape(LENGTH, DIM),
        pairs.reshape(2, LENGTH, DIM),
    )
    moved = scatter(relaid.reshape(64, LOCAL, DIM))
    return moved.reshape(queries.shape)


def solution(mesh):
    return jax.shard_map(
        per_device,
        mesh=mesh,
        in_specs=(P("pp", None, None, "cp", None), P("pp", None, None, None, "cp", None), P(), P()),
        out_specs=P("pp", None, None, "cp", None),
        check_vma=False,
    )
```

time: 307 us -> 148 us (0.48)
  Pallas kernels: 0 us -> 142 us
  waiting for transfers between devices: 111 us -> 0 us
  other arithmetic: 53.7 us -> 1.1 us
  blocking collectives: 48.5 us -> 0 us
  local copies, waits for them, and re-layouts: 36.4 us -> 4.53 us
  starting transfers between devices: 27.9 us -> 0 us
  matrix products: 25.8 us -> 0 us
    pallas_call x0 -> x3, Pallas kernels: none -> 142 us  [the longest x1 70.8 us: gather(): pl.pallas_call(gather_kernel, out_shape=(jax.ShapeDtypeStruct((64, LOCAL,...]
    all_to_all x2 -> x0, waiting for transfers between devices: 83.8 us -> none  [the longest x1 52.6 us: per_device(): lax.all_to_all(copied.reshape(2, cp_devices, local_rows, head_width), 'cp...]
    all_to_all x1 -> x0, blocking collectives: 48.5 us -> none  [per_device(): lax.all_to_all(relaid, 'cp', split_axis=1, concat_axis=0, tiled=True)]
    ppermute x1 -> x0, waiting for transfers between devices: 26.8 us -> none  [from_behind(): return lax.ppermute(value, axis, pairs)]
    all_to_all x2 -> x0, starting transfers between devices: 26 us -> none  [the longest x1 17.8 us: per_device(): lax.all_to_all(sent_queries, 'cp', split_axis=0, concat_axis=1, tiled=True)]
    dot_general x72 -> x0, matrix products: 25.8 us -> none  [the longest x36 14.2 us: key_step(): jnp.einsum('hqk,kd->hqd', weights.astype(jnp.bfloat16), value_part, prefe...]
    unnamed x1 -> x0, other arithmetic: 22.4 us -> none
    another operation x2 -> x0, other arithmetic: 17.3 us -> none
  transfers between devices with their start and end apart: 3 -> 0, of which waited for: 3 -> 0; matrix products, arithmetic and copies ran while one was open for 5% -> 0% of each run, Pallas kernels for 0% -> 0%
where the time goes in v1:
time: 148 us
  Pallas kernels  142 us (96%)
  local copies, waits for them, and re-layouts  4.53 us (3%)
    pallas_call x1, Pallas kernels, gather(): pl.pallas_call(gather_kernel, out_shape=(jax.ShapeDtypeStruct((64, LOCAL,...  70.8 us
    pallas_call x1, Pallas kernels, scatter(): pl.pallas_call(scatter_kernel, out_shape=jax.ShapeDtypeStruct((64, LOCAL,...  51.1 us
    pallas_call x1, Pallas kernels, attend(): pl.pallas_call(functools.partial(attend_kernel, bq=bq, bk=bk), out_shape=...  20.5 us
    unnamed x9, local copies, waits for them, and re-layouts  4.45 us

profile of v1, /device:TPU:1, one launch (start us, length us, event | category | flops | bytes accessed | tf_op | source)
XLA Modules:
  0.0 148.2 jit_solution(501596968451131001)
XLA Ops:
  0.0 0.7 dynamic-slice_multiply_fusion
  0.7 0.1 add_convert_fusion
  0.8 0.1 convert_element_type.11
  0.9 0.2 fusion
  1.1 0.1 pad_maximum_fusion
  1.2 0.0 copy-start
  1.2 1.2 copy-done
  2.4 0.0 copy-start.1
  2.4 0.9 copy-done.1
  3.4 70.8 %gather.1 = (bf16[64,64,128]{2,1,0:T(8,128)(2,1)S(1)}, bf16[2,4,2,8,64,128]{5,4,3,2,1,0:T(8,128)(2,1)S(1)}) custom-call(bf16[64,64,128]{2,1,0:T(8,128)(2,1)S(1)} %bitcast.10, bf16[2,8,64,128]{3,2,1,0:T(8,128)(2,1)S(1)} %bitcast.11, f32[64,128]{1,0:T(8,128)S(1)} %get-tuple-element.12.cos_ref, f32[64,128]{1,0:T(8,128)S(1)} %get-tuple-element.13.sin_ref), custom_call_target="tpu_custom_call" | custom-call | tf_op jit(solution)/shard_map/gather/pallas_call | solution.py:135
  74.2 0.0 copy-start.2
  74.2 0.6 copy-done.2
  74.8 0.0 copy-start.3
  74.8 0.7 copy-done.3
  75.5 20.5 %attend.1 = bf16[4096,128]{1,0:T(8,128)(2,1)S(1)} custom-call(s32[128]{0:T(128)S(1)} %copy-done.2, s32[128]{0:T(128)S(1)} %copy-done.3, bf16[4096,128]{1,0:T(8,128)(2,1)S(1)} %bitcast.9, bf16[2,4096,128]{2,1,0:T(8,128)(2,1)S(1)} %bitcast.8), custom_call_target="tpu_custom_call" | custom-call | tf_op jit(solution)/shard_map/attend/pallas_call | solution.py:270
  96.0 51.1 %scatter.1 = bf16[64,64,128]{2,1,0:T(8,128)(2,1)S(1)} custom-call(bf16[64,64,128]{2,1,0:T(8,128)(2,1)S(1)} %bitcast.6), custom_call_target="tpu_custom_call" | custom-call | tf_op jit(solution)/shard_map/scatter/pallas_call | solution.py:180
  147.2 1.0 copy.6
  (1 shorter events, 0.0 us)
Async XLA Ops:
  1.2 1.2 copy-start
  2.4 0.9 copy-start.1
  74.2 0.7 copy-start.2
  74.8 0.7 copy-start.3

commit v2 on v0

v2 whole, which is shorter than its diff:
```python
import math
import random

import jax
import jax.numpy as jnp
from jax import lax
from jax.experimental import pallas as pl
from jax.experimental.pallas import tpu as pltpu
from jax.sharding import PartitionSpec as P

MESH = pl.DeviceIdType.MESH
F32 = jnp.float32
BF16 = jnp.bfloat16
LENGTH = 4096
DIM = 128
BLOCKS = 128
ROWS = 32
LOCAL = 64
YS, ZS = 4, 8
CHIPS = YS * ZS
SECTIONS = 8
VROWS = 144
TILE = 1024
TB = TILE // ROWS


def steps_of(seed):
    rest = [(dy, dz) for dy in range(YS) for dz in range(ZS)]
    random.Random(seed).shuffle(rest)
    hops_y = {0: 0, 1: 2, 2: 4, 3: 2}
    total, order = [0, 0], []
    while rest:
        share = 64 * (len(order) + 1) / 32

        def cost(step):
            along_z = total[0] + min(step[1], ZS - step[1])
            along_y = total[1] + hops_y[step[0]]
            return (along_z - share) ** 2 + (along_y - share) ** 2

        best = min(rest, key=cost)
        rest.remove(best)
        order.append(best)
        total[0] += min(best[1], ZS - best[1])
        total[1] += hops_y[best[0]]
    return order


def turned(x, cos, sin):
    wide = x.astype(F32)
    return (wide * cos + pltpu.roll(wide, 64, wide.ndim - 1) * sin).astype(BF16)


def layer_kernel(
    kv_block, q_block, new_block, q_ref, kv_ref, cos_ref, sin_ref, o_ref,
    qs, kvs, okv, qa, qb, oa, ob, ra, rb, k2, vt, seq, qt, acc, mx,
    q_send, q_recv, z_send, z_recv, y_send, y_recv, c_send, c_recv,
    x_send, x_recv, t_send, t_recv, o_send, o_recv, loc,
):
    pp = lax.axis_index("pp")
    me = lax.axis_index("cp")
    y, z, c = me // 16, lax.rem(me // 2, ZS), lax.rem(me, 2)
    chip = y * ZS + z
    ahead, behind = lax.rem(pp + 1, SECTIONS), lax.rem(pp + SECTIONS - 1, SECTIONS)
    other = 1 - c

    def at(dy, dz, core):
        return (lax.rem(y + dy + YS, YS) * ZS + lax.rem(z + dz + ZS, ZS)) * 2 + core

    sign = 1 - 2 * c

    def mirrored(step):
        return lax.rem(y + sign * step[0] + YS, YS), lax.rem(z + sign * step[1] + ZS, ZS)

    def device(place):
        return (place[0] * ZS + place[1]) * 2 + c

    q_steps = [s for s in steps_of(1) if s != (0, 0)]
    o_steps = steps_of(2)

    barrier = pltpu.get_barrier_semaphore()
    for s in q_steps:
        pl.semaphore_signal(barrier, inc=1, device_id=(pp, device(mirrored(s))), device_id_type=MESH)
    pl.semaphore_signal(barrier, inc=1, device_id=(pp, at(0, 0, other)), device_id_type=MESH)
    for s in o_steps:
        pl.semaphore_signal(barrier, inc=1, device_id=(behind, device(mirrored(s))), device_id_type=MESH)

    cos, sin = cos_ref[...], sin_ref[...]

    def turn_keys(j, carry):
        kvs[0, j] = turned(kv_ref[0, j], cos, sin).reshape(2, ROWS, DIM)
        kvs[1, j] = kv_ref[1, j].reshape(2, ROWS, DIM)
        return carry

    lax.fori_loop(0, 8, turn_keys, 0)
    pl.semaphore_wait(barrier, 64)

    def remote(src, dst, send, recv, dev, section=pp):
        copy = pltpu.make_async_remote_copy(
            src_ref=src, dst_ref=dst, send_sem=send, recv_sem=recv,
            device_id=(section, dev), device_id_type=MESH,
        )
        copy.start()
        return copy

    def plane(at_y):
        return (at_y * 2 + c) * 16

    z_copies = []
    for n, dz in enumerate((4, 3, 5, 2, 6, 1, 7)):
        z_copies.append(remote(
            kvs.at[:, lax.rem(z + dz, ZS)], okv.at[:, pl.ds(plane(y) + 2 * z, 2)],
            z_send.at[n], z_recv.at[n], at(0, dz, c),
        ))
    own = pltpu.make_async_copy(kvs.at[:, z], okv.at[:, pl.ds(plane(y) + 2 * z, 2)], loc.at[0])
    own.start()

    held = (qa, qb)
    slot_of = (c * CHIPS + chip) * 2
    q_copies = ([], [])

    def send_queries(head, first, last):
        for n in range(first, last):
            to = mirrored(q_steps[n])
            item = to[1] * 8 + to[0] * 2 + head
            qs[item] = turned(q_ref[item], cos, sin).reshape(2, ROWS, DIM)
            q_copies[head].append(remote(
                qs.at[item], held[head].at[pl.ds(slot_of, 2)], q_send.at[head, n], q_recv.at[head, n], device(to)
            ))

    def keep_queries(head):
        item = z * 8 + y * 2 + head
        held[head][pl.ds(slot_of, 2)] = turned(q_ref[item], cos, sin).reshape(2, ROWS, DIM)

    send_queries(0, 0, 12)
    keep_queries(0)
    keep_queries(1)
    for copy in z_copies:
        copy.wait_recv()
    own.wait()
    part = okv.at[:, pl.ds(plane(y), 16)]
    up = remote(part, part, y_send.at[0], y_recv.at[0], at(1, 0, c))
    down = remote(part, part, y_send.at[1], y_recv.at[1], at(YS - 1, 0, c))
    core = [remote(part, part, c_send.at[0], c_recv.at[0], at(0, 0, other))]
    send_queries(0, 12, 31)
    below, above, far = lax.rem(y + 3, YS), lax.rem(y + 1, YS), lax.rem(y + 2, YS)
    up.wait_recv()
    keys = okv.at[0, pl.ds(plane(below), 16)]
    up2 = remote(keys, keys, y_send.at[2], y_recv.at[2], at(1, 0, c))
    part = okv.at[:, pl.ds(plane(below), 16)]
    core.append(remote(part, part, c_send.at[1], c_recv.at[1], at(0, 0, other)))
    down.wait_recv()
    values = okv.at[1, pl.ds(plane(above), 16)]
    down2 = remote(values, values, y_send.at[3], y_recv.at[3], at(YS - 1, 0, c))
    part = okv.at[:, pl.ds(plane(above), 16)]
    core.append(remote(part, part, c_send.at[2], c_recv.at[2], at(0, 0, other)))
    send_queries(1, 0, 31)
    up2.wait_recv()
    down2.wait_recv()
    part = okv.at[:, pl.ds(plane(far), 16)]
    core.append(remote(part, part, c_send.at[3], c_recv.at[3], at(0, 0, other)))
    for copy in core:
        copy.wait()
    for copy in z_copies + [up, down, up2, down2]:
        copy.wait_send()

    def arrange(b, carry):
        dst = pl.ds(pl.multiple_of(b * ROWS, ROWS), ROWS)
        keys = okv[0, kv_block[b]]
        k2[dst, 0:DIM] = keys
        k2[dst, DIM : 2 * DIM] = keys
        seq[dst, :] = okv[1, kv_block[b]]
        return carry

    lax.fori_loop(0, BLOCKS, arrange, 0, unroll=8)
    for j in range(LENGTH // 512):
        vt[0:DIM, j * 512 : (j + 1) * 512] = seq[j * 512 : (j + 1) * 512, :].T
    vt[DIM:VROWS, :] = jnp.ones((VROWS - DIM, LENGTH), BF16)

    scale = math.log2(math.e) / math.sqrt(DIM)
    tiles = (c, 3 - c)

    def attend(head, out):
        for copy in q_copies[head]:
            copy.wait_recv()
        mine = held[head].at[pl.ds(c * 2 * CHIPS, 2 * CHIPS)]
        swap = remote(mine, mine, x_send.at[head], x_recv.at[head], at(0, 0, other))
        swap.wait()
        t_copies = []
        for slot in range(2):
            tile = tiles[slot]

            def pick(b, carry):
                seq[pl.ds(pl.multiple_of(b * ROWS, ROWS), ROWS), :] = held[head][q_block[tile * TB + b]]
                return carry

            lax.fori_loop(0, TB, pick, 0, unroll=8)
            for j in range(TILE // 512):
                cols = slice(j * 512, (j + 1) * 512)
                x = seq[cols, :].astype(F32) * scale
                high = x.astype(BF16)
                low = (x - high.astype(F32)).astype(BF16)
                qt[0:DIM, cols] = high.T
                qt[DIM : 2 * DIM, cols] = low.T

            def block(k0, first):
                s = jnp.dot(k2[pl.ds(k0, TILE), :], qt[...], preferred_element_type=F32)
                if first:
                    key = lax.broadcasted_iota(jnp.int32, s.shape, 0)
                    query = lax.broadcasted_iota(jnp.int32, s.shape, 1)
                    s = jnp.where(key <= query, s, -1e30)
                top = jnp.max(s, axis=0, keepdims=True)
                if not first:
                    before = mx[...]
                    top = jnp.maximum(before, top)
                weights = jnp.exp2(s - top).astype(BF16)
                summed = jnp.dot(vt[:, pl.ds(k0, TILE)], weights, preferred_element_type=F32)
                if not first:
                    summed = acc[...] * jnp.exp2(before - top) + summed
                acc[...] = summed
                mx[...] = top

            block(pl.multiple_of(tile * TILE, TILE), True)

            def body(j, carry):
                block(pl.multiple_of(j * TILE, TILE), False)
                return carry

            lax.fori_loop(0, tile, body, 0)
            rows = pl.ds(tile * TB, TB)
            out[rows] = (acc[0:DIM, :] / acc[DIM : DIM + 1, :]).T.astype(BF16).reshape(TB, ROWS, DIM)
            done = out.at[rows]
            t_copies.append(remote(
                done, done, t_send.at[head, slot], t_recv.at[head, slot], at(0, 0, other)
            ))
        for copy in t_copies:
            copy.wait()

    def hand_on(head, out, relaid):
        def relay(b, carry):
            j = (b // 2) * 4 + 2 * c + lax.rem(b, 2)
            relaid[b] = out[new_block[j]]
            return carry

        lax.fori_loop(0, 2 * CHIPS, relay, 0, unroll=8)
        copies = []
        for n, s in enumerate(o_steps):
            to = mirrored(s)
            rows = pl.ds((to[0] * ZS + to[1]) * 2, 2)
            copies.append(remote(
                relaid.at[rows], o_ref.at[z * 8 + y * 2 + head],
                o_send.at[head, n], o_recv.at[head, n], device(to), ahead,
            ))
        return copies

    attend(0, oa)
    o_copies = hand_on(0, oa, ra)
    attend(1, ob)
    o_copies += hand_on(1, ob, rb)
    for copy in q_copies[0] + q_copies[1]:
        copy.wait_send()
    for copy in o_copies:
        copy.wait()


def layer(kv_block, q_block, new_block, queries, pairs, cos, sin):
    vmem = pl.BlockSpec(memory_space=pltpu.VMEM)
    smem = pl.BlockSpec(memory_space=pltpu.SMEM)
    dma = pltpu.SemaphoreType.DMA
    buf = pltpu.VMEM
    return pl.pallas_call(
        layer_kernel,
        out_shape=jax.ShapeDtypeStruct((64, 2, ROWS, DIM), BF16),
        in_specs=[smem] * 3 + [vmem] * 4,
        out_specs=pl.BlockSpec(memory_space=pl.ANY),
        scratch_shapes=[
            buf((64, 2, ROWS, DIM), BF16),
            buf((2, 8, 2, ROWS, DIM), BF16),
            buf((2, BLOCKS, ROWS, DIM), BF16),
            buf((BLOCKS, ROWS, DIM), BF16),
            buf((BLOCKS, ROWS, DIM), BF16),
            buf((BLOCKS, ROWS, DIM), BF16),
            buf((BLOCKS, ROWS, DIM), BF16),
            buf((BLOCKS // 2, ROWS, DIM), BF16),
            buf((BLOCKS // 2, ROWS, DIM), BF16),
            buf((LENGTH, 2 * DIM), BF16),
            buf((VROWS, LENGTH), BF16),
            buf((LENGTH, DIM), BF16),
            buf((2 * DIM, TILE), BF16),
            buf((VROWS, TILE), F32),
            buf((1, TILE), F32),
            dma((2, 31)), dma((2, 31)), dma((7,)), dma((7,)), dma((4,)), dma((4,)), dma((4,)), dma((4,)),
            dma((2,)), dma((2,)), dma((2, 2)), dma((2, 2)), dma((2, 32)), dma((2, 32)), dma((1,)),
        ],
        compiler_params=pltpu.CompilerParams(
            collective_id=1, has_side_effects=True, vmem_limit_bytes=50 * 2**20
        ),
        name="layer",
    )(kv_block, q_block, new_block, queries, pairs, cos, sin)


def per_device(queries, keys_values, old_block, new_block):
    me = lax.axis_index("cp")
    two = lax.dynamic_slice_in_dim(old_block, me * 2, 2)
    token = (two[:, None] * ROWS + jnp.arange(ROWS, dtype=jnp.int32)[None, :]).reshape(LOCAL)
    spacing = jnp.arange(DIM // 2, dtype=F32) * (2.0 / DIM)
    inverse = jnp.exp(-spacing * jnp.log(F32(1000000.0)))
    angles = token.astype(F32)[:, None] * inverse[None, :]
    cosine, sine = jnp.cos(angles), jnp.sin(angles)
    cos = jnp.concatenate([cosine, cosine], axis=1)
    sin = jnp.concatenate([-sine, sine], axis=1)
    j = jnp.arange(BLOCKS, dtype=jnp.int32)
    y, z, c, half = j // 32, (j // 4) % 8, (j // 2) % 2, j % 2
    kv_place = ((y * 2 + c) * ZS + z) * 2 + half
    q_place = ((c * YS + y) * ZS + z) * 2 + half
    holds = old_block[None, :] == j[:, None]
    kv_block = jnp.sum(jnp.where(holds, kv_place[None, :], 0), axis=1)
    q_block = jnp.sum(jnp.where(holds, q_place[None, :], 0), axis=1)
    moved = layer(
        kv_block, q_block, new_block,
        queries.reshape(64, LOCAL, DIM), keys_values.reshape(2, 8, LOCAL, DIM), cos, sin,
    )
    return moved.reshape(queries.shape)


def solution(mesh):
    return jax.shard_map(
        per_device,
        mesh=mesh,
        in_specs=(P("pp", None, None, "cp", None), P("pp", None, None, None, "cp", None), P(), P()),
        out_specs=P("pp", None, None, "cp", None),
        check_vma=False,
    )
```

time: 307 us -> 128 us (0.42)
  the two profiles are of different devices: /device:TPU:1 before, /device:TPU:6 now
where the time goes in v2:
time: 128 us
  Pallas kernels  123 us (96%)
  local copies, waits for them, and re-layouts  2.93 us (2%)
  other arithmetic  1.92 us (2%)
    pallas_call x1, Pallas kernels, layer(): pl.pallas_call(layer_kernel, out_shape=jax.ShapeDtypeStruct((64, 2, ROWS,...  123 us
    unnamed x7, local copies, waits for them, and re-layouts  2.84 us

profile of v2, /device:TPU:6, one launch (start us, length us, event | category | flops | bytes accessed | tf_op | source)
XLA Modules:
  0.0 128.2 jit_solution(12799108272718717199)
XLA Ops:
  0.0 0.0 copy-start.1
  0.0 0.8 dynamic-slice_multiply_fusion
  0.8 0.1 add_convert_fusion
  0.8 0.1 convert_element_type.11
  1.0 0.8 select_reduce_fusion
  1.7 0.2 fusion
  1.9 0.1 pad_maximum_fusion
  2.0 0.0 copy-start.2
  2.0 0.0 copy-done.1
  2.0 0.6 copy-done.2
  2.7 0.0 copy-start
  2.7 1.2 copy-done
  3.9 123.3 %layer.1 = bf16[64,2,32,128]{3,2,1,0:T(8,128)(2,1)S(1)} custom-call(s32[128]{0:T(128)S(1)} %get-tuple-element.6.kv_block, s32[128]{0:T(128)S(1)} %get-tuple-element.5.q_block, s32[128]{0:T(128)S(1)} %copy-done.2, bf16[64,64,128]{2,1,0:T(8,128)(2,1)S(1)} %bitcast.4, bf16[2,8,64,128]{3,2,1,0:T(8,128)(2,1)S(1)} %bitcast.5, ...), custom_call_target="tpu_custom_call" | custom-call | tf_op jit(solution)/shard_map/layer/pallas_call | solution.py:270
  127.2 1.0 copy.6
  (2 shorter events, 0.0 us)
Async XLA Ops:
  0.0 2.0 %copy-start.1 = (bf16[1,2,2,4,64,128]{5,4,3,2,1,0:T(8,128)(2,1)S(1)}, bf16[1,2,2,4,64,128]{5,4,3,2,1,0:T(8,128)(2,1)}, u32[]{:S(2)}) copy-start(bf16[1,2,2,4,64,128]{5,4,3,2,1,0:T(8,128)(2,1)} %param.5) | copy-start | bytes 786436
  2.0 0.7 copy-start.2
  2.7 1.2 copy-start

commit v3 on v2

v3 whole, which is shorter than its diff:
```python
import math

import jax
import jax.numpy as jnp
from jax import lax
from jax.experimental import pallas as pl
from jax.experimental.pallas import tpu as pltpu
from jax.sharding import PartitionSpec as P

MESH = pl.DeviceIdType.MESH
F32 = jnp.float32
BF16 = jnp.bfloat16
LENGTH = 4096
DIM = 128
BLOCKS = 128
ROWS = 32
LOCAL = 64
YS, ZS = 4, 8
CHIPS = YS * ZS
SECTIONS = 8
VROWS = 144
TILE = 1024
TB = TILE // ROWS
Z_ORDER = (1, 7, 3, 5, 2, 6, 4)
ODD, EVEN = (1, 7, 3, 5), (2, 6, 4, 0)


def turned(x, cos, sin):
    wide = x.astype(F32)
    return (wide * cos + pltpu.roll(wide, 64, wide.ndim - 1) * sin).astype(BF16)


def layer_kernel(
    kv_block, q_block, new_block, q_ref, kv_ref, cos_ref, sin_ref, o_ref,
    qs, qz, qa, qb, kvs, kz, okv, oa, ob, ra, rb, oz, k2, vt, seq, qt, acc, mx, sent, got, loc,
):
    pp = lax.axis_index("pp")
    me = lax.axis_index("cp")
    y, z, c = me // 16, lax.rem(me // 2, ZS), lax.rem(me, 2)
    ahead, behind = lax.rem(pp + 1, SECTIONS), lax.rem(pp + SECTIONS - 1, SECTIONS)
    other = 1 - c
    parity = lax.rem(z, 2)
    sign = 1 - 2 * c

    def along_z(dz):
        return lax.rem(z + sign * dz + ZS, ZS)

    def along_y(dy):
        return lax.rem(y + sign * dy + YS, YS)

    def device(at_y, at_z, core=c):
        return (at_y * ZS + at_z) * 2 + core

    barrier = pltpu.get_barrier_semaphore()
    greeted = [(pp, device(y, along_z(dz))) for dz in range(1, ZS)]
    greeted += [(pp, device(along_y(dy), z)) for dy in range(1, YS)]
    greeted += [(pp, device(y, z, other))]
    greeted += [(behind, device(along_y(dy), z)) for dy in range(YS)]
    for place in greeted:
        pl.semaphore_signal(barrier, inc=1, device_id=place, device_id_type=MESH)

    cos, sin = cos_ref[...], sin_ref[...]

    def turn_keys(j, carry):
        kvs[0, j] = turned(kv_ref[0, j], cos, sin).reshape(2, ROWS, DIM)
        kvs[1, j] = kv_ref[1, j].reshape(2, ROWS, DIM)
        return carry

    lax.fori_loop(0, 8, turn_keys, 0)
    pl.semaphore_wait(barrier, len(greeted))

    count = [0, 0]

    def remote(src, dst, dev, section=pp):
        copy = pltpu.make_async_remote_copy(
            src_ref=src, dst_ref=dst, send_sem=sent.at[count[0]], recv_sem=got.at[count[0]],
            device_id=(section, dev), device_id_type=MESH,
        )
        count[0] += 1
        copy.start()
        return copy

    def local(src, dst):
        copy = pltpu.make_async_copy(src, dst, loc.at[count[1]])
        count[1] += 1
        copy.start()
        return copy

    outgoing = []

    ky = [
        remote(kvs.at[:, pl.ds(2 * along_y(dy), 2)], kz.at[:, :, pl.ds(2 * y, 2)], device(along_y(dy), z))
        for dy in (2, 1, 3)
    ]
    ky_own = local(kvs.at[:, pl.ds(2 * y, 2)], kz.at[:, :, pl.ds(2 * y, 2)])

    held = (qa, qb)

    def turn_queries(head, at_z, out):
        def one(at_y, carry):
            item = (2 * at_y + lax.rem(at_z, 2)) * 8 + (at_z // 2) * 2 + head
            out[at_y] = turned(q_ref[item], cos, sin).reshape(2, ROWS, DIM)
            return carry

        lax.fori_loop(0, YS, one, 0, unroll=True)

    def queries_along_z(head):
        copies = {}
        for dz in Z_ORDER:
            to = along_z(dz)
            turn_queries(head, to, qs.at[head, to])
            copies[dz] = remote(qs.at[head, to], qz.at[head, parity, z // 2], device(y, to))
        turn_queries(head, z, qz.at[head, parity, z // 2])
        return copies

    def queries_along_y(head, steps, copies):
        which = lax.rem(parity + steps[0], 2)
        for dz in steps:
            if dz:
                copies[dz].wait_recv()
        place = held[head].at[pl.ds((c * YS + y) * ZS + which * 4, 4)]
        return [
            remote(qz.at[head, which, :, along_y(dy)], place, device(along_y(dy), z)) for dy in (2, 1, 3)
        ], local(qz.at[head, which, :, y], place)

    za = queries_along_z(0)
    for copy in ky:
        copy.wait_recv()
    ky_own.wait()

    def part(at_z, half=None):
        block = c * ZS + at_z
        return okv.at[:, block] if half is None else okv.at[half, block]

    def near(dz):
        return remote(kz.at[:, lax.rem(parity + dz, 2)], part(z), device(y, along_z(dz)))

    def pass_on(came, to, half=None):
        ref = part(along_z(came), half)
        return remote(ref, ref, device(y, along_z(to)))

    one_up, one_down = near(1), near(7)
    two_up, two_down = near(2), near(6)
    kz_own = local(kz.at[:, parity], part(z))
    one_up.wait_recv()
    three_up = pass_on(7, 2)
    one_down.wait_recv()
    three_down = pass_on(1, 6)
    zb = queries_along_z(1)
    ya, ya_own = queries_along_y(0, ODD, za)
    two_up.wait_recv()
    four_up = pass_on(6, 2, 0)
    two_down.wait_recv()
    four_down = pass_on(2, 6, 1)
    more, more_own = queries_along_y(0, EVEN, za)
    ya += more
    for copy in (three_up, three_down, four_up, four_down):
        copy.wait_recv()
    kz_own.wait()
    half_kv = okv.at[:, pl.ds(c * ZS, ZS)]
    kv_swap = remote(half_kv, half_kv, device(y, z, other))
    for copy in ya:
        copy.wait_recv()
    ya_own.wait()
    more_own.wait()

    def swap_queries(head):
        half_q = held[head].at[pl.ds(c * CHIPS, CHIPS)]
        return remote(half_q, half_q, device(y, z, other))

    q_swap = swap_queries(0)
    kv_swap.wait()
    outgoing += ky + list(za.values()) + list(zb.values()) + ya
    outgoing += [one_up, one_down, two_up, two_down, three_up, three_down, four_up, four_down]

    def arrange(b, carry):
        dst = pl.ds(pl.multiple_of(b * ROWS, ROWS), ROWS)
        at = kv_block[b]
        keys = okv[0, at // 8, lax.rem(at, 8)]
        k2[dst, 0:DIM] = keys
        k2[dst, DIM : 2 * DIM] = keys
        seq[dst, :] = okv[1, at // 8, lax.rem(at, 8)]
        return carry

    lax.fori_loop(0, BLOCKS, arrange, 0, unroll=8)
    for j in range(LENGTH // 512):
        vt[0:DIM, j * 512 : (j + 1) * 512] = seq[j * 512 : (j + 1) * 512, :].T
    vt[DIM:VROWS, :] = jnp.ones((VROWS - DIM, LENGTH), BF16)

    scale = math.log2(math.e) / math.sqrt(DIM)
    tiles = (c, 3 - c)

    def attend(head, out, between):
        t_copies = []
        for slot in range(2):
            tile = tiles[slot]

            def pick(b, carry):
                at = q_block[tile * TB + b]
                seq[pl.ds(pl.multiple_of(b * ROWS, ROWS), ROWS), :] = held[head][at // 2, lax.rem(at, 2)]
                return carry

            lax.fori_loop(0, TB, pick, 0, unroll=8)
            for j in range(TILE // 512):
                cols = slice(j * 512, (j + 1) * 512)
                x = seq[cols, :].astype(F32) * scale
                high = x.astype(BF16)
                low = (x - high.astype(F32)).astype(BF16)
                qt[0:DIM, cols] = high.T
                qt[DIM : 2 * DIM, cols] = low.T

            def block(k0, first):
                s = jnp.dot(k2[pl.ds(k0, TILE), :], qt[...], preferred_element_type=F32)
                if first:
                    key = lax.broadcasted_iota(jnp.int32, s.shape, 0)
                    query = lax.broadcasted_iota(jnp.int32, s.shape, 1)
                    s = jnp.where(key <= query, s, -1e30)
                top = jnp.max(s, axis=0, keepdims=True)
                if not first:
                    before = mx[...]
                    top = jnp.maximum(before, top)
                weights = jnp.exp2(s - top).astype(BF16)
                summed = jnp.dot(vt[:, pl.ds(k0, TILE)], weights, preferred_element_type=F32)
                if not first:
                    summed = acc[...] * jnp.exp2(before - top) + summed
                acc[...] = summed
                mx[...] = top

            block(pl.multiple_of(tile * TILE, TILE), True)

            def body(j, carry):
                block(pl.multiple_of(j * TILE, TILE), False)
                return carry

            lax.fori_loop(0, tile, body, 0)
            rows = pl.ds(tile * TB, TB)
            out[rows] = (acc[0:DIM, :] / acc[DIM : DIM + 1, :]).T.astype(BF16).reshape(TB, ROWS, DIM)
            done = out.at[rows]
            t_copies.append(remote(done, done, device(y, z, other)))
            if slot == 0:
                between()
        for copy in t_copies:
            copy.wait()

    def hand_on(head, out, relaid):
        def relay(b, carry):
            j = ((lax.rem(b // 2, YS) * ZS + b // 8) * 2 + c) * 2 + lax.rem(b, 2)
            relaid[b // 8, lax.rem(b // 2, YS), lax.rem(b, 2)] = out[new_block[j]]
            return carry

        lax.fori_loop(0, 2 * CHIPS, relay, 0, unroll=8)
        copies = {}
        for dz in Z_ORDER:
            to = along_z(dz)
            copies[dz] = remote(relaid.at[to], oz.at[head, parity, z // 2], device(y, to))
        return copies, local(relaid.at[z], oz.at[head, parity, z // 2])

    def to_next(head, steps, copies, own):
        which = lax.rem(parity + steps[0], 2)
        for dz in steps:
            if dz:
                copies[dz].wait_recv()
            else:
                own.wait()
        return [
            remote(
                oz.at[head, which, :, along_y(dy)], o_ref.at[y, which, :, head],
                device(along_y(dy), z), ahead,
            )
            for dy in (1, 3, 2, 0)
        ]

    yb, yb_own = queries_along_y(1, ODD, zb)
    more, more_own = queries_along_y(1, EVEN, zb)
    yb += more
    outgoing += yb
    q_swap.wait()
    attend(0, oa, lambda: None)
    oza, oza_own = hand_on(0, oa, ra)
    for copy in yb:
        copy.wait_recv()
    yb_own.wait()
    more_own.wait()
    q_swap = swap_queries(1)
    q_swap.wait()
    final = []

    def first_to_next():
        final.extend(to_next(0, ODD, oza, oza_own))
        final.extend(to_next(0, EVEN, oza, oza_own))

    attend(1, ob, first_to_next)
    ozb, ozb_own = hand_on(1, ob, rb)
    final += to_next(1, ODD, ozb, ozb_own)
    final += to_next(1, EVEN, ozb, ozb_own)
    outgoing += list(oza.values()) + list(ozb.values())
    for copy in outgoing:
        copy.wait_send()
    for copy in final:
        copy.wait()


def layer(kv_block, q_block, new_block, queries, pairs, cos, sin):
    vmem = pl.BlockSpec(memory_space=pltpu.VMEM)
    smem = pl.BlockSpec(memory_space=pltpu.SMEM)
    dma = pltpu.SemaphoreType.DMA
    buf = pltpu.VMEM
    return pl.pallas_call(
        layer_kernel,
        out_shape=jax.ShapeDtypeStruct((YS, 2, 4, 2, 2, ROWS, DIM), BF16),
        in_specs=[smem] * 3 + [vmem] * 4,
        out_specs=pl.BlockSpec(memory_space=pl.ANY),
        scratch_shapes=[
            buf((2, ZS, YS, 2, ROWS, DIM), BF16),
            buf((2, 2, 4, YS, 2, ROWS, DIM), BF16),
            buf((64, 2, ROWS, DIM), BF16),
            buf((64, 2, ROWS, DIM), BF16),
            buf((2, 8, 2, ROWS, DIM), BF16),
            buf((2, 2, 8, ROWS, DIM), BF16),
            buf((2, 16, 8, ROWS, DIM), BF16),
            buf((BLOCKS, ROWS, DIM), BF16),
            buf((BLOCKS, ROWS, DIM), BF16),
            buf((ZS, YS, 2, ROWS, DIM), BF16),
            buf((ZS, YS, 2, ROWS, DIM), BF16),
            buf((2, 2, 4, YS, 2, ROWS, DIM), BF16),
            buf((LENGTH, 2 * DIM), BF16),
            buf((VROWS, LENGTH), BF16),
            buf((LENGTH, DIM), BF16),
            buf((2 * DIM, TILE), BF16),
            buf((VROWS, TILE), F32),
            buf((1, TILE), F32),
            dma((80,)), dma((80,)), dma((10,)),
        ],
        compiler_params=pltpu.CompilerParams(
            collective_id=1, has_side_effects=True, vmem_limit_bytes=50 * 2**20
        ),
        name="layer",
    )(kv_block, q_block, new_block, queries, pairs, cos, sin)


def per_device(queries, keys_values, old_block, new_block):
    me = lax.axis_index("cp")
    two = lax.dynamic_slice_in_dim(old_block, me * 2, 2)
    token = (two[:, None] * ROWS + jnp.arange(ROWS, dtype=jnp.int32)[None, :]).reshape(LOCAL)
    spacing = jnp.arange(DIM // 2, dtype=F32) * (2.0 / DIM)
    inverse = jnp.exp(-spacing * jnp.log(F32(1000000.0)))
    angles = token.astype(F32)[:, None] * inverse[None, :]
    cosine, sine = jnp.cos(angles), jnp.sin(angles)
    cos = jnp.concatenate([cosine, cosine], axis=1)
    sin = jnp.concatenate([-sine, sine], axis=1)
    j = jnp.arange(BLOCKS, dtype=jnp.int32)
    y, z, c, half = j // 32, (j // 4) % 8, (j // 2) % 2, j % 2
    kv_place = ((c * ZS + z) * YS + y) * 2 + half
    q_place = ((c * YS + y) * ZS + (z % 2) * 4 + z // 2) * 2 + half
    holds = old_block[None, :] == j[:, None]
    kv_block = jnp.sum(jnp.where(holds, kv_place[None, :], 0), axis=1)
    q_block = jnp.sum(jnp.where(holds, q_place[None, :], 0), axis=1)
    moved = layer(
        kv_block, q_block, new_block,
        queries.reshape(64, LOCAL, DIM), keys_values.reshape(2, 8, LOCAL, DIM), cos, sin,
    )
    return moved.reshape(queries.shape)


def solution(mesh):
    return jax.shard_map(
        per_device,
        mesh=mesh,
        in_specs=(P("pp", None, None, "cp", None), P("pp", None, None, None, "cp", None), P(), P()),
        out_specs=P("pp", None, None, "cp", None),
        check_vma=False,
    )
```

time: 128 us -> 126 us (0.984)
  the two profiles are of different devices: /device:TPU:6 before, /device:TPU:1 now
where the time goes in v3:
time: 126 us
  Pallas kernels  121 us (96%)
  local copies, waits for them, and re-layouts  2.93 us (2%)
  other arithmetic  1.92 us (2%)
    pallas_call x1, Pallas kernels, layer(): pl.pallas_call(layer_kernel, out_shape=jax.ShapeDtypeStruct((YS, 2, 4, 2,...  121 us
    unnamed x7, local copies, waits for them, and re-layouts  2.84 us

profile of v3, /device:TPU:1, one launch (start us, length us, event | category | flops | bytes accessed | tf_op | source)
XLA Modules:
  0.0 126.2 jit_solution(15578409626623380625)
XLA Ops:
  0.0 0.0 copy-start.1
  0.0 0.8 dynamic-slice_multiply_fusion
  0.8 0.1 add_convert_fusion
  0.8 0.1 convert_element_type.11
  1.0 0.8 select_reduce_fusion
  1.7 0.2 fusion
  1.9 0.1 pad_maximum_fusion
  2.0 0.0 copy-start.2
  2.0 0.0 copy-done.1
  2.1 0.6 copy-done.2
  2.7 0.0 copy-start
  2.7 1.2 copy-done
  3.9 121.3 %layer.1 = bf16[4,2,4,2,2,32,128]{6,5,4,3,2,1,0:T(8,128)(2,1)S(1)} custom-call(s32[128]{0:T(128)S(1)} %get-tuple-element.6.kv_block, s32[128]{0:T(128)S(1)} %get-tuple-element.5.q_block, s32[128]{0:T(128)S(1)} %copy-done.2, bf16[64,64,128]{2,1,0:T(8,128)(2,1)S(1)} %bitcast.4, bf16[2,8,64,128]{3,2,1,0:T(8,128)(2,1)S(1)} %bitcast.5, ...), custom_call_target="tpu_custom_call" | custom-call | tf_op jit(solution)/shard_map/layer/pallas_call | solution.py:308
  125.2 1.0 copy.6
  (2 shorter events, 0.0 us)
Async XLA Ops:
  0.0 2.0 %copy-start.1 = (bf16[1,2,2,4,64,128]{5,4,3,2,1,0:T(8,128)(2,1)S(1)}, bf16[1,2,2,4,64,128]{5,4,3,2,1,0:T(8,128)(2,1)}, u32[]{:S(2)}) copy-start(bf16[1,2,2,4,64,128]{5,4,3,2,1,0:T(8,128)(2,1)} %param.5) | copy-start | bytes 786436
  2.0 0.7 copy-start.2
  2.7 1.2 copy-start

commit v4 on v3

v4 whole, which is shorter than its diff:
```python
import math
import random

import jax
import jax.numpy as jnp
from jax import lax
from jax.experimental import pallas as pl
from jax.experimental.pallas import tpu as pltpu
from jax.sharding import PartitionSpec as P

MESH = pl.DeviceIdType.MESH
F32 = jnp.float32
BF16 = jnp.bfloat16
LENGTH = 4096
DIM = 128
BLOCKS = 128
ROWS = 32
LOCAL = 64
YS, ZS = 4, 8
CHIPS = YS * ZS
SECTIONS = 8
VROWS = 144
TILE = 1024
TB = TILE // ROWS
PARTS = 2
WIDE = TILE // PARTS
Z_ORDER = (1, 7, 3, 5, 2, 6, 4)
ODD, EVEN = (1, 7, 3, 5), (2, 6, 4, 0)


def steps_of(seed):
    rest = [(dy, dz) for dy in range(YS) for dz in range(ZS)]
    random.Random(seed).shuffle(rest)
    hops_y = {0: 0, 1: 2, 2: 4, 3: 2}
    total, order = [0, 0], []
    while rest:
        share = 64 * (len(order) + 1) / 32

        def cost(step):
            along_z = total[0] + min(step[1], ZS - step[1])
            along_y = total[1] + hops_y[step[0]]
            return (along_z - share) ** 2 + (along_y - share) ** 2

        best = min(rest, key=cost)
        rest.remove(best)
        order.append(best)
        total[0] += min(best[1], ZS - best[1])
        total[1] += hops_y[best[0]]
    return order


def turned(x, cos, sin):
    wide = x.astype(F32)
    return (wide * cos + pltpu.roll(wide, 64, wide.ndim - 1) * sin).astype(BF16)


def layer_kernel(
    old_block, new_block, old_ref, q_hbm, kv_hbm, o_ref,
    q_ref, kv_ref, table, kv_block, q_block, qs, qz, qa, qb, kvs, kz, okv, oa, ob, ra, rb, k2, vt, seq, qt, acc, mx, sent, got, loc, ready,
):
    pp = lax.axis_index("pp")
    me = lax.axis_index("cp")
    y, z, c = me // 16, lax.rem(me // 2, ZS), lax.rem(me, 2)
    ahead, behind = lax.rem(pp + 1, SECTIONS), lax.rem(pp + SECTIONS - 1, SECTIONS)
    other = 1 - c
    parity = lax.rem(z, 2)
    sign = 1 - 2 * c

    def along_z(dz):
        return lax.rem(z + sign * dz + ZS, ZS)

    def along_y(dy):
        return lax.rem(y + sign * dy + YS, YS)

    def device(at_y, at_z, core=c):
        return (at_y * ZS + at_z) * 2 + core

    load_kv = pltpu.make_async_copy(kv_hbm, kv_ref, loc.at[10])
    load_kv.start()
    load_q = pltpu.make_async_copy(q_hbm, q_ref, loc.at[11])
    load_q.start()
    barrier = pltpu.get_barrier_semaphore()
    greeted = [(pp, device(y, along_z(dz))) for dz in range(1, ZS)]
    greeted += [(pp, device(along_y(dy), z)) for dy in range(1, YS)]
    greeted += [(pp, device(y, z, other))]
    greeted += [(ahead, me)]
    for place in greeted:
        pl.semaphore_signal(barrier, inc=1, device_id=place, device_id_type=MESH)

    lane = lax.broadcasted_iota(jnp.int32, (LOCAL, DIM), 1)
    row = lax.broadcasted_iota(jnp.int32, (LOCAL, DIM), 0)
    block = jnp.where(row < ROWS, old_block[2 * me], old_block[2 * me + 1])
    token = (block * ROWS + lax.rem(row, ROWS)).astype(F32)
    spacing = lax.rem(lane, DIM // 2).astype(F32) * (2.0 / DIM)
    angle = token * jnp.exp(-spacing * math.log(1000000.0))
    cos = jnp.cos(angle)
    sin = jnp.where(lane < DIM // 2, -jnp.sin(angle), jnp.sin(angle))

    j = lax.broadcasted_iota(jnp.int32, (BLOCKS, BLOCKS), 0)
    holds = old_ref[...] == lax.broadcasted_iota(jnp.int32, (BLOCKS, BLOCKS), 1)
    jy, jz, jc, half = j // 32, lax.rem(j // 4, ZS), lax.rem(j // 2, 2), lax.rem(j, 2)
    kv_place = ((jc * ZS + jz) * YS + jy) * 2 + half
    q_place = ((jc * YS + jy) * ZS + lax.rem(jz, 2) * 4 + jz // 2) * 2 + half
    table[0:1, :] = jnp.max(jnp.where(holds, kv_place, 0), axis=0, keepdims=True)
    table[1:2, :] = jnp.max(jnp.where(holds, q_place, 0), axis=0, keepdims=True)
    kv_table = pltpu.make_async_copy(table.at[pl.ds(0, 1)], kv_block, loc.at[12])
    kv_table.start()
    q_table = pltpu.make_async_copy(table.at[pl.ds(1, 1)], q_block, loc.at[13])
    q_table.start()
    load_kv.wait()

    def turn_keys(j, carry):
        kvs[0, j] = turned(kv_ref[0, j], cos, sin).reshape(2, ROWS, DIM)
        kvs[1, j] = kv_ref[1, j].reshape(2, ROWS, DIM)
        return carry

    lax.fori_loop(0, 8, turn_keys, 0)
    kv_table.wait()
    q_table.wait()
    load_q.wait()
    pl.semaphore_wait(barrier, len(greeted))

    count = [0, 0]

    def remote(src, dst, dev, section=pp):
        copy = pltpu.make_async_remote_copy(
            src_ref=src, dst_ref=dst, send_sem=sent.at[count[0]], recv_sem=got.at[count[0]],
            device_id=(section, dev), device_id_type=MESH,
        )
        count[0] += 1
        copy.start()
        return copy

    def local(src, dst):
        copy = pltpu.make_async_copy(src, dst, loc.at[count[1]])
        count[1] += 1
        copy.start()
        return copy

    outgoing = []

    ky = [
        remote(kvs.at[:, pl.ds(2 * along_y(dy), 2)], kz.at[:, :, pl.ds(2 * y, 2)], device(along_y(dy), z))
        for dy in (2, 1, 3)
    ]
    ky_own = local(kvs.at[:, pl.ds(2 * y, 2)], kz.at[:, :, pl.ds(2 * y, 2)])

    held = (qa, qb)

    def turn_queries(head, at_z, out):
        def one(at_y, carry):
            item = (2 * at_y + lax.rem(at_z, 2)) * 8 + (at_z // 2) * 2 + head
            out[at_y] = turned(q_ref[item], cos, sin).reshape(2, ROWS, DIM)
            return carry

        lax.fori_loop(0, YS, one, 0, unroll=True)

    def queries_along_z(head):
        copies = {}
        for dz in Z_ORDER:
            to = along_z(dz)
            turn_queries(head, to, qs.at[head, to])
            copies[dz] = remote(qs.at[head, to], qz.at[head, parity, z // 2], device(y, to))
        turn_queries(head, z, qz.at[head, parity, z // 2])
        return copies

    def queries_along_y(head, steps, copies):
        which = lax.rem(parity + steps[0], 2)
        for dz in steps:
            if dz:
                copies[dz].wait_recv()
        place = held[head].at[pl.ds((c * YS + y) * ZS + which * 4, 4)]
        return [
            remote(qz.at[head, which, :, along_y(dy)], place, device(along_y(dy), z)) for dy in (2, 1, 3)
        ], local(qz.at[head, which, :, y], place)

    za = queries_along_z(0)
    for copy in ky:
        copy.wait_recv()
    ky_own.wait()

    def part(at_z, half=None):
        block = c * ZS + at_z
        return okv.at[:, block] if half is None else okv.at[half, block]

    def near(dz):
        return remote(kz.at[:, lax.rem(parity + dz, 2)], part(z), device(y, along_z(dz)))

    def pass_on(came, to, half=None):
        ref = part(along_z(came), half)
        return remote(ref, ref, device(y, along_z(to)))

    one_up, one_down = near(1), near(7)
    two_up, two_down = near(2), near(6)
    kz_own = local(kz.at[:, parity], part(z))
    one_up.wait_recv()
    three_up = pass_on(7, 2)
    one_down.wait_recv()
    three_down = pass_on(1, 6)
    ya, ya_own = queries_along_y(0, ODD, za)
    two_up.wait_recv()
    four_up = pass_on(6, 2, 0)
    two_down.wait_recv()
    four_down = pass_on(2, 6, 1)
    more, more_own = queries_along_y(0, EVEN, za)
    ya += more
    zb = queries_along_z(1)
    for copy in (three_up, three_down, four_up, four_down):
        copy.wait_recv()
    kz_own.wait()
    half_kv = okv.at[:, pl.ds(c * ZS, ZS)]
    kv_swap = remote(half_kv, half_kv, device(y, z, other))
    for copy in ya:
        copy.wait_recv()
    ya_own.wait()
    more_own.wait()
    pl.semaphore_signal(ready, inc=1, device_id=(behind, me), device_id_type=MESH)

    def swap_queries(head):
        half_q = held[head].at[pl.ds(c * CHIPS, CHIPS)]
        return remote(half_q, half_q, device(y, z, other))

    q_swap = swap_queries(0)
    kv_swap.wait()
    outgoing += ky + list(za.values()) + list(zb.values()) + ya
    outgoing += [one_up, one_down, two_up, two_down, three_up, three_down, four_up, four_down]

    def arrange(b, carry):
        dst = pl.ds(pl.multiple_of(b * ROWS, ROWS), ROWS)
        at = kv_block[0, b]
        keys = okv[0, at // 8, lax.rem(at, 8)]
        k2[dst, 0:DIM] = keys
        k2[dst, DIM : 2 * DIM] = keys
        seq[dst, :] = okv[1, at // 8, lax.rem(at, 8)]
        return carry

    lax.fori_loop(0, BLOCKS, arrange, 0, unroll=8)
    for j in range(LENGTH // 512):
        vt[0:DIM, j * 512 : (j + 1) * 512] = seq[j * 512 : (j + 1) * 512, :].T
    vt[DIM:VROWS, :] = jnp.ones((VROWS - DIM, LENGTH), BF16)

    scale = math.log2(math.e) / math.sqrt(DIM)
    tiles = (c, 3 - c)

    def attend(head, out):
        t_copies = []
        for slot in range(2):
            tile = tiles[slot]

            def pick(b, carry):
                at = q_block[0, tile * TB + b]
                seq[pl.ds(pl.multiple_of(b * ROWS, ROWS), ROWS), :] = held[head][at // 2, lax.rem(at, 2)]
                return carry

            lax.fori_loop(0, TB, pick, 0, unroll=8)
            for j in range(TILE // 512):
                cols = slice(j * 512, (j + 1) * 512)
                x = seq[cols, :].astype(F32) * scale
                high = x.astype(BF16)
                low = (x - high.astype(F32)).astype(BF16)
                qt[0:DIM, cols] = high.T
                qt[DIM : 2 * DIM, cols] = low.T

            def score(k0, part, width):
                keys = k2[pl.ds(k0, width), :]
                return jnp.dot(keys, qt[:, part * WIDE : (part + 1) * WIDE], preferred_element_type=F32)

            def blend(k0, width, weights):
                return jnp.dot(vt[:, pl.ds(k0, width)], weights, preferred_element_type=F32)

            own = pl.multiple_of(tile * TILE, TILE)
            ahead_of = score(own, 0, WIDE)
            for part in range(PARTS):
                s, width = ahead_of, (part + 1) * WIDE
                if part + 1 < PARTS:
                    ahead_of = score(own, part + 1, width + WIDE)
                key = lax.broadcasted_iota(jnp.int32, s.shape, 0)
                query = lax.broadcasted_iota(jnp.int32, s.shape, 1)
                s = jnp.where(key <= query + part * WIDE, s, -1e30)
                top = jnp.max(s, axis=0, keepdims=True)
                cols = slice(part * WIDE, width)
                acc[:, cols] = blend(own, width, jnp.exp2(s - top).astype(BF16))
                mx[:, cols] = top

            def body(j, carry):
                k0 = pl.multiple_of(j * TILE, TILE)
                before, total = mx[...], acc[...]
                ahead_of = score(k0, 0, TILE)
                for part in range(PARTS):
                    s = ahead_of
                    if part + 1 < PARTS:
                        ahead_of = score(k0, part + 1, TILE)
                    cols = slice(part * WIDE, (part + 1) * WIDE)
                    top = jnp.maximum(before[:, cols], jnp.max(s, axis=0, keepdims=True))
                    summed = blend(k0, TILE, jnp.exp2(s - top).astype(BF16))
                    acc[:, cols] = total[:, cols] * jnp.exp2(before[:, cols] - top) + summed
                    mx[:, cols] = top
                return carry

            lax.fori_loop(0, tile, body, 0)
            rows = pl.ds(tile * TB, TB)
            out[rows] = (acc[0:DIM, :] / acc[DIM : DIM + 1, :]).T.astype(BF16).reshape(TB, ROWS, DIM)
            done = out.at[rows]
            t_copies.append(remote(done, done, device(y, z, other)))
        for copy in t_copies:
            copy.wait()

    o_steps = steps_of(2)

    def hand_on(head, out, relaid):
        item = ((y * 2 + parity) * 4 + z // 2) * 2 + head
        copies = []
        for dy, dz in o_steps:
            to_y, to_z = along_y(dy), along_z(dz)
            chip = to_y * ZS + to_z
            for half in range(2):
                relaid[chip, half] = out[new_block[(chip * 2 + c) * 2 + half]]
            copies.append(remote(relaid.at[chip], o_ref.at[item], device(to_y, to_z), ahead))
        return copies

    yb, yb_own = queries_along_y(1, ODD, zb)
    more, more_own = queries_along_y(1, EVEN, zb)
    yb += more
    outgoing += yb
    q_swap.wait()
    attend(0, oa)
    pl.semaphore_wait(ready, 1)
    final = hand_on(0, oa, ra)
    for copy in yb:
        copy.wait_recv()
    yb_own.wait()
    more_own.wait()
    q_swap = swap_queries(1)
    q_swap.wait()
    attend(1, ob)
    final += hand_on(1, ob, rb)
    for copy in outgoing:
        copy.wait_send()
    for copy in final:
        copy.wait()


def layer(old_block, new_block, queries, pairs):
    vmem = pl.BlockSpec(memory_space=pltpu.VMEM)
    smem = pl.BlockSpec(memory_space=pltpu.SMEM)
    hbm = pl.BlockSpec(memory_space=pl.ANY)
    dma = pltpu.SemaphoreType.DMA
    buf = pltpu.VMEM
    return pl.pallas_call(
        layer_kernel,
        out_shape=jax.ShapeDtypeStruct((64, 2, ROWS, DIM), BF16),
        in_specs=[smem, smem, vmem, hbm, hbm],
        out_specs=hbm,
        scratch_shapes=[
            buf((64, LOCAL, DIM), BF16),
            buf((2, 8, LOCAL, DIM), BF16),
            buf((8, BLOCKS), jnp.int32),
            pltpu.SMEM((1, BLOCKS), jnp.int32),
            pltpu.SMEM((1, BLOCKS), jnp.int32),
            buf((2, ZS, YS, 2, ROWS, DIM), BF16),
            buf((2, 2, 4, YS, 2, ROWS, DIM), BF16),
            buf((64, 2, ROWS, DIM), BF16),
            buf((64, 2, ROWS, DIM), BF16),
            buf((2, 8, 2, ROWS, DIM), BF16),
            buf((2, 2, 8, ROWS, DIM), BF16),
            buf((2, 16, 8, ROWS, DIM), BF16),
            buf((BLOCKS, ROWS, DIM), BF16),
            buf((BLOCKS, ROWS, DIM), BF16),
            buf((CHIPS, 2, ROWS, DIM), BF16),
            buf((CHIPS, 2, ROWS, DIM), BF16),
            buf((LENGTH, 2 * DIM), BF16),
            buf((VROWS, LENGTH), BF16),
            buf((LENGTH, DIM), BF16),
            buf((2 * DIM, TILE), BF16),
            buf((VROWS, TILE), F32),
            buf((1, TILE), F32),
            dma((112,)), dma((112,)), dma((14,)), pltpu.SemaphoreType.REGULAR,
        ],
        compiler_params=pltpu.CompilerParams(
            collective_id=1, has_side_effects=True, vmem_limit_bytes=50 * 2**20
        ),
        name="layer",
    )(old_block, new_block, old_block[:, None], queries, pairs)


def per_device(queries, keys_values, old_block, new_block):
    moved = layer(
        old_block, new_block, queries.reshape(64, LOCAL, DIM), keys_values.reshape(2, 8, LOCAL, DIM)
    )
    return moved.reshape(queries.shape)


def solution(mesh):
    return jax.shard_map(
        per_device,
        mesh=mesh,
        in_specs=(P("pp", None, None, "cp", None), P("pp", None, None, None, "cp", None), P(), P()),
        out_specs=P("pp", None, None, "cp", None),
        check_vma=False,
    )
```

time: 126 us -> 106 us (0.84)
  Pallas kernels: 121 us -> 101 us
  other arithmetic: 1.92 us -> 0 us
  local copies, waits for them, and re-layouts: 2.93 us -> 4.46 us
    pallas_call x1, Pallas kernels: 121 us -> 101 us  [layer(): pl.pallas_call(layer_kernel, out_shape=jax.ShapeDtypeStruct((64, 2, ROWS,...]
    unnamed x7 -> x9, local copies, waits for them, and re-layouts: 2.84 us -> 4.34 us
where the time goes in v4:
time: 106 us
  Pallas kernels  101 us (95%)
  local copies, waits for them, and re-layouts  4.46 us (4%)
    pallas_call x1, Pallas kernels, layer(): pl.pallas_call(layer_kernel, out_shape=jax.ShapeDtypeStruct((64, 2, ROWS,...  101 us
    unnamed x9, local copies, waits for them, and re-layouts  4.34 us

profile of v4, /device:TPU:1, one launch (start us, length us, event | category | flops | bytes accessed | tf_op | source)
XLA Modules:
  0.0 105.5 jit_solution(10868236411886464892)
XLA Ops:
  0.0 0.0 copy-start.2
  0.0 0.7 copy-done.2
  0.7 0.0 copy-start.3
  0.7 0.1 copy.5.old_ref
  0.8 0.5 copy-done.3
  1.3 0.0 copy-start
  1.3 1.2 %copy-done = bf16[1,2,32,64,128]{4,3,2,1,0:T(8,128)(2,1)S(1)} copy-done((bf16[1,2,32,64,128]{4,3,2,1,0:T(8,128)(2,1)S(1)}, bf16[1,2,32,64,128]{4,3,2,1,0:T(8,128)(2,1)}, u32[]{:S(2)}) %copy-start) | copy-done | bytes 1048600
  2.5 0.0 copy-start.1
  2.5 0.9 copy-done.1
  3.5 101.1 %layer.1 = bf16[64,2,32,128]{3,2,1,0:T(8,128)(2,1)S(1)} custom-call(s32[128]{0:T(128)S(1)} %copy-done.2, s32[128]{0:T(128)S(1)} %copy-done.3, s32[128,1]{1,0:T(8,128)S(1)} %copy.5.old_ref, bf16[64,64,128]{2,1,0:T(8,128)(2,1)S(1)} %bitcast.5, bf16[2,8,64,128]{3,2,1,0:T(8,128)(2,1)S(1)} %bitcast.6), custom_call_target="tpu_custom_call" | custom-call | tf_op jit(solution)/shard_map/layer/pallas_call | solution.py:349
  104.6 1.0 copy.7
Async XLA Ops:
  0.0 0.7 copy-start.2
  0.7 0.7 copy-start.3
  1.3 1.2 %copy-start = (bf16[1,2,32,64,128]{4,3,2,1,0:T(8,128)(2,1)S(1)}, bf16[1,2,32,64,128]{4,3,2,1,0:T(8,128)(2,1)}, u32[]{:S(2)}) copy-start(bf16[1,2,32,64,128]{4,3,2,1,0:T(8,128)(2,1)} %param.4) | copy-start | bytes 3145732
  2.5 0.9 copy-start.1

commit v5 on v4

--- a/solution.py
+++ b/solution.py
@@ -96,13 +96,14 @@
     cos = jnp.cos(angle)
     sin = jnp.where(lane < DIM // 2, -jnp.sin(angle), jnp.sin(angle))
 
-    j = lax.broadcasted_iota(jnp.int32, (BLOCKS, BLOCKS), 0)
-    holds = old_ref[...] == lax.broadcasted_iota(jnp.int32, (BLOCKS, BLOCKS), 1)
+    j = lax.broadcasted_iota(jnp.int32, (BLOCKS, BLOCKS), 1)
+    holds = old_ref[...] == lax.broadcasted_iota(jnp.int32, (BLOCKS, BLOCKS), 0)
     jy, jz, jc, half = j // 32, lax.rem(j // 4, ZS), lax.rem(j // 2, 2), lax.rem(j, 2)
     kv_place = ((jc * ZS + jz) * YS + jy) * 2 + half
     q_place = ((jc * YS + jy) * ZS + lax.rem(jz, 2) * 4 + jz // 2) * 2 + half
-    table[0:1, :] = jnp.max(jnp.where(holds, kv_place, 0), axis=0, keepdims=True)
-    table[1:2, :] = jnp.max(jnp.where(holds, q_place, 0), axis=0, keepdims=True)
+    for n, where in enumerate((kv_place, q_place)):
+        found = jnp.max(jnp.where(holds, where, 0), axis=1, keepdims=True)
+        table[n : n + 1, :] = jnp.broadcast_to(found, (BLOCKS, BLOCKS)).T[0:1, :]
     kv_table = pltpu.make_async_copy(table.at[pl.ds(0, 1)], kv_block, loc.at[12])
     kv_table.start()
     q_table = pltpu.make_async_copy(table.at[pl.ds(1, 1)], q_block, loc.at[13])
@@ -222,6 +223,7 @@
 
     q_swap = swap_queries(0)
     kv_swap.wait()
+    yb, yb_own = queries_along_y(1, ODD, zb)
     outgoing += ky + list(za.values()) + list(zb.values()) + ya
     outgoing += [one_up, one_down, two_up, two_down, three_up, three_down, four_up, four_down]
 
@@ -318,19 +320,18 @@
             copies.append(remote(relaid.at[chip], o_ref.at[item], device(to_y, to_z), ahead))
         return copies
 
-    yb, yb_own = queries_along_y(1, ODD, zb)
     more, more_own = queries_along_y(1, EVEN, zb)
     yb += more
     outgoing += yb
     q_swap.wait()
     attend(0, oa)
     pl.semaphore_wait(ready, 1)
-    final = hand_on(0, oa, ra)
     for copy in yb:
         copy.wait_recv()
     yb_own.wait()
     more_own.wait()
     q_swap = swap_queries(1)
+    final = hand_on(0, oa, ra)
     q_swap.wait()
     attend(1, ob)
     final += hand_on(1, ob, rb)
@@ -377,10 +378,10 @@
             dma((112,)), dma((112,)), dma((14,)), pltpu.SemaphoreType.REGULAR,
         ],
         compiler_params=pltpu.CompilerParams(
-            collective_id=1, has_side_effects=True, vmem_limit_bytes=50 * 2**20
+            collective_id=1, has_side_effects=True, vmem_limit_bytes=63 * 2**20
         ),
         name="layer",
-    )(old_block, new_block, old_block[:, None], queries, pairs)
+    )(old_block, new_block, old_block[None, :], queries, pairs)
 
 
 def per_device(queries, keys_values, old_block, new_block):

time: 106 us -> 102 us (0.962)
  local copies, waits for them, and re-layouts: 4.46 us -> 2.26 us
  Pallas kernels: 101 us -> 99.5 us
    unnamed x9 -> x1, local copies, waits for them, and re-layouts: 4.34 us -> 2.26 us
    pallas_call x1, Pallas kernels: 101 us -> 99.5 us  [layer(): pl.pallas_call(layer_kernel, out_shape=jax.ShapeDtypeStruct((64, 2, ROWS,...]
where the time goes in v5:
time: 102 us
  Pallas kernels  99.5 us (98%)
  local copies, waits for them, and re-layouts  2.26 us (2%)
    pallas_call x1, Pallas kernels, layer(): pl.pallas_call(layer_kernel, out_shape=jax.ShapeDtypeStruct((64, 2, ROWS,...  99.5 us
    unnamed x1, local copies, waits for them, and re-layouts  2.26 us

profile of v5, /device:TPU:1, one launch (start us, length us, event | category | flops | bytes accessed | tf_op | source)
XLA Modules:
  0.0 101.8 jit_solution(18113966267871169365)
XLA Ops:
  0.0 99.5 %layer.1 = bf16[64,2,32,128]{3,2,1,0:T(8,128)(2,1)} custom-call(s32[128]{0:T(128)} %old_block.1, s32[128]{0:T(128)} %new_block.1, s32[1,128]{1,0:T(1,128)} %bitcast.7, bf16[64,64,128]{2,1,0:T(8,128)(2,1)} %bitcast.5, bf16[2,8,64,128]{3,2,1,0:T(8,128)(2,1)} %bitcast.6), custom_call_target="tpu_custom_call" | custom-call | tf_op jit(solution)/shard_map/layer/pallas_call | solution.py:350
  99.5 2.3 %copy.6 = bf16[1,2,32,64,128]{4,3,2,1,0:T(8,128)(2,1)} copy(bf16[1,2,32,64,128]{4,3,2,1,0:T(8,128)(2,1)} %bitcast.4) | data formatting | bytes 2097152

commit v6 on v5

--- a/solution.py
+++ b/solution.py
@@ -378,7 +378,7 @@
             dma((112,)), dma((112,)), dma((14,)), pltpu.SemaphoreType.REGULAR,
         ],
         compiler_params=pltpu.CompilerParams(
-            collective_id=1, has_side_effects=True, vmem_limit_bytes=63 * 2**20
+            collective_id=1, has_side_effects=True, vmem_limit_bytes=62 * 2**20
         ),
         name="layer",
     )(old_block, new_block, old_block[None, :], queries, pairs)

time: 102 us -> 102 us (level)
  no operation moved by 1% of the time
where the time goes in v6:
time: 102 us
  Pallas kernels  99.5 us (98%)
  local copies, waits for them, and re-layouts  2.26 us (2%)
    pallas_call x1, Pallas kernels, layer(): pl.pallas_call(layer_kernel, out_shape=jax.ShapeDtypeStruct((64, 2, ROWS,...  99.5 us
    unnamed x1, local copies, waits for them, and re-layouts  2.26 us

profile of v6, /device:TPU:1, one launch (start us, length us, event | category | flops | bytes accessed | tf_op | source)
XLA Modules:
  0.0 101.8 jit_solution(18113966267871169365)
XLA Ops:
  0.0 99.5 %layer.1 = bf16[64,2,32,128]{3,2,1,0:T(8,128)(2,1)} custom-call(s32[128]{0:T(128)} %old_block.1, s32[128]{0:T(128)} %new_block.1, s32[1,128]{1,0:T(1,128)} %bitcast.7, bf16[64,64,128]{2,1,0:T(8,128)(2,1)} %bitcast.5, bf16[2,8,64,128]{3,2,1,0:T(8,128)(2,1)} %bitcast.6), custom_call_target="tpu_custom_call" | custom-call | tf_op jit(solution)/shard_map/layer/pallas_call | solution.py:350
  99.5 2.3 %copy.6 = bf16[1,2,32,64,128]{4,3,2,1,0:T(8,128)(2,1)} copy(bf16[1,2,32,64,128]{4,3,2,1,0:T(8,128)(2,1)} %bitcast.4) | data formatting | bytes 2097152
